TPU v7x, 32 devices: a whole 2x2x4 slice. The times are simulated.
32 devices in a mesh: outer: 2 (over x), sec: 8 (over z, core), tp: 2 (over y).
Axes of the slice: x: 2, y: 2, z: 4, core: 2. Of those that a mesh axis runs over, the one named last changes fastest.
Arguments:
- tile_maps: bfloat16 [32, 12, 12, 3072], P(('outer', 'sec'), None, None, 'tp'), may hold values from -6 to 6
- tile_shape: int32 [32, 2], P(('outer', 'sec')), may hold values from 4 to 12
- conv_kernel: float32 [7, 7, 3072], P(None, None, 'tp'), may hold values from -0.875 to 0.875
- norm_gain: float32 [3072], P('tp'), may hold values from 0.25 to 1.75
- norm_bias: float32 [3072], P('tp'), may hold values from -3 to 3
- projector: bfloat16 [3072, 7168], P('tp', 'sec'), may hold values from -0.109375 to 0.109375
- text_rows: bfloat16 [9216, 7168], P(('outer', 'sec'), 'tp'), may hold values from -6 to 6
- row_order: int32 [16, 576], P(('outer', 'sec')), may hold values from 0 to 575, each once within a row
- seq_gain: float32 [7168], P('tp'), may hold values from 0.25 to 1.75
- cotangent: bfloat16 [9216, 7168], P(('outer', 'sec'), 'tp'), may hold values from -0.2772166 to 0.2772166, as said below
Outputs:
- normed: bfloat16 [9216, 7168], P(('outer', 'sec'), 'tp')
- kernel_delta: float32 [7, 7, 3072], P(None, None, 'tp')
- gain_delta: float32 [3072], P('tp')
- bias_delta: float32 [3072], P('tp')
Inputs may be any that keep to these rules, and one draw needn't show every extreme that they name: `row_order`: each row lists where the visual tokens arriving at that device stand, in arrival order, then the text rows. `tile_shape`: valid rows and columns of each tile, the rest of the map is padding. `cotangent`: gradient of the training loss.
All inputs are finite; a program needn't handle non-finite values.
Results may differ from a plain program's by a relative error of at most 0.0043.
Values may be sent and summed in bfloat16 or wider, within the bound.
A program may use at most 128 MiB of HBM per device.

v0:
```python
import jax
import jax.numpy as jnp
from jax import lax
from jax.sharding import PartitionSpec as P


def shape_mask(tile_shape, grid):
    places = lax.broadcasted_iota(jnp.int32, (1, grid), 1)
    rows_ok = places < tile_shape[:, 0:1]
    cols_ok = places < tile_shape[:, 1:2]
    return (rows_ok[:, :, None] & cols_ok[:, None, :]).astype(jnp.float32)


def on_device(
    tile_maps,
    tile_shape,
    conv_kernel,
    norm_gain,
    norm_bias,
    projector,
    text_rows,
    row_order,
    seq_gain,
    cotangent,
):
    grid = tile_maps.shape[1]
    half_ch = tile_maps.shape[3]
    channels = half_ch * lax.axis_size("tp")
    rows_dev = tile_maps.shape[0] * grid * grid
    width = text_rows.shape[1] * lax.axis_size("tp")
    validity = shape_mask(tile_shape, grid)[..., None]
    masked = tile_maps.astype(jnp.float32) * validity
    padded = jnp.pad(masked, ((0, 0), (3, 3), (3, 3), (0, 0)))
    conv_out = jnp.zeros(masked.shape, jnp.float32)
    for row_off in range(7):
        for col_off in range(7):
            conv_out = (
                conv_out
                + padded[:, row_off : row_off + grid, col_off : col_off + grid, :]
                * conv_kernel[row_off, col_off]
            )
    total_one, total_two = lax.psum(
        (jnp.sum(conv_out, axis=-1), jnp.sum(conv_out * conv_out, axis=-1)), "tp"
    )
    center = (total_one / channels)[..., None]
    inverse = lax.rsqrt((total_two / channels)[..., None] - center * center + 1e-06)
    normal = (conv_out - center) * inverse
    features = (
        (validity * (normal * norm_gain + norm_bias))
        .astype(jnp.bfloat16)
        .reshape(rows_dev, half_ch)
    )
    whole_weight = lax.all_gather(projector, "sec", axis=1, tiled=True)
    partial_value = jnp.dot(features, whole_weight, preferred_element_type=jnp.float32)
    visual = lax.psum_scatter(partial_value, "tp", scatter_dimension=1, tiled=True).astype(
        jnp.bfloat16
    )
    arrived = lax.all_to_all(visual, "sec", split_axis=0, concat_axis=0, tiled=True)
    positions = row_order[0, :rows_dev]
    merged = text_rows.at[positions].set(arrived)
    wide = merged.astype(jnp.float32)
    upstream = cotangent.astype(jnp.float32) * seq_gain
    square_sum, along = lax.psum(
        (jnp.sum(wide * wide, axis=-1), jnp.sum(upstream * wide, axis=-1)), "tp"
    )
    inv_rms = lax.rsqrt(square_sum / width + 1e-05)[:, None]
    normed = (wide * inv_rms * seq_gain).astype(jnp.bfloat16)
    grad_seq = inv_rms * upstream - wide * (inv_rms * inv_rms * inv_rms) * along[:, None] / width
    picked = grad_seq[positions].astype(jnp.bfloat16)
    returned = lax.all_to_all(picked, "sec", split_axis=0, concat_axis=0, tiled=True)
    full_grad = lax.all_gather(returned, "tp", axis=1, tiled=True)
    grad_rows = jnp.dot(full_grad, whole_weight.T, preferred_element_type=jnp.float32)
    masked_grad = grad_rows.reshape(masked.shape) * validity
    scaled = masked_grad * norm_gain
    first_sum, second_sum = lax.psum(
        (jnp.sum(scaled, axis=-1), jnp.sum(scaled * normal, axis=-1)), "tp"
    )
    grad_conv = inverse * (
        scaled - (first_sum / channels)[..., None] - normal * (second_sum / channels)[..., None]
    )
    kernel_rows = []
    for row_off in range(7):
        for col_off in range(7):
            window = padded[:, row_off : row_off + grid, col_off : col_off + grid, :]
            kernel_rows.append(jnp.sum(window * grad_conv, axis=(0, 1, 2)))
    gain_grad = jnp.sum(masked_grad * normal, axis=(0, 1, 2))
    bias_grad = jnp.sum(masked_grad, axis=(0, 1, 2))
    local_delta = jnp.stack(kernel_rows + [gain_grad, bias_grad], axis=0)
    pods = lax.axis_size("outer")
    entries = 51 * channels
    pod_sum = lax.psum(local_delta, "sec")
    norm_sq = lax.psum(jnp.sum(pod_sum * pod_sum), "tp")
    factor = jnp.minimum(1.0, 1.0 / jnp.sqrt(norm_sq / entries + 1e-06))
    average = lax.psum(pod_sum * factor, "outer") / pods
    return (normed, average[:49].reshape(7, 7, half_ch), average[49], average[50])


def solution(mesh):
    in_specs = (
        P(("outer", "sec"), None, None, "tp"),
        P(("outer", "sec"), None),
        P(None, None, "tp"),
        P("tp"),
        P("tp"),
        P("tp", "sec"),
        P(("outer", "sec"), "tp"),
        P(("outer", "sec"), None),
        P("tp"),
        P(("outer", "sec"), "tp"),
    )
    out_specs = (P(("outer", "sec"), "tp"), P(None, None, "tp"), P("tp"), P("tp"))
    return jax.shard_map(
        on_device, mesh=mesh, in_specs=in_specs, out_specs=out_specs, check_vma=False
    )
```

profile of v0, /device:TPU:1, one launch (start us, length us, event | category | flops | bytes accessed | tf_op | source)
XLA Modules:
  0.0 696.3 jit_solution(15552070662868830435)
XLA Ops:
  7.2 4.4 copy.23
  11.7 0.6 copy-done.9
  12.3 0.2 slice_reduce_fusion.52
  12.5 0.1 copy-done.2
  12.6 0.2 slice_reduce_fusion.48
  12.8 0.3 slice_reduce_fusion.50
  13.1 0.9 slice_reduce_fusion.49
  14.2 0.2 convert_multiply_fusion.5
  14.4 23.6 %fusion.8 = (f32[2,12,12]{2,1,0:T(8,128)S(1)}, f32[2,12,12]{2,1,0:T(8,128)S(1)}, f32[2,12,12,1536]{3,2,1,0:T(8,128)}) fusion(f32[1536]{0:T(1024)S(1)} %get-tuple-element.110, f32[1536]{0:T(1024)S(1)} %get-tuple-element.111, f32[1536]{0:T(1024)S(1)} %get-tuple-element.64, f32[1536]{0:T(1024)S(1)} %get-tuple-element.65, f32[1536]{0:T(1024)S(1)} %get-tuple-element.66, ...), kind=kLoop, calls=%fused_computation.189 | loop fusion | flops 44236224 | bytes 3842304 | tf_op jit(solution)/shard_map/reduce_sum | solution.py:43
  38.1 8.0 %all-reduce.3 = (f32[2,12,12]{2,1,0:T(8,128)S(1)}, f32[2,12,12]{2,1,0:T(8,128)S(1)}) all-reduce(f32[2,12,12]{2,1,0:T(8,128)S(1)} %get-tuple-element.58, f32[2,12,12]{2,1,0:T(8,128)S(1)} %get-tuple-element.57), channel_id=1, replica_groups=mesh['outer'=2,'sec'=8,'tp'=2] {'tp'}, use_global_device_ids=true, to_apply=%region_3.4 | all-reduce | flops 576 | bytes 4608 | tf_op jit(solution)/shard_map/psum | solution.py:42
  46.1 0.6 copy-done.3
  46.7 3.5 multiply_convert_fusion
  50.2 1.1 reshape.168
  51.4 157.0 %all-gather.3.cloned.1.call-done = bf16[1536,7168]{1,0:T(8,128)(2,1)} async-done(((bf16[1536,896]{1,0:T(8,128)(2,1)}), bf16[1536,7168]{1,0:T(8,128)(2,1)}) %all-gather.3.cloned.1.call-update) | async-done | bytes 22020112 | tf_op jit(solution)/shard_map/all_gather | solution.py:53
  208.3 13.1 %fusion.9 = f32[288,7168]{1,0:T(8,128)} fusion(bf16[288,1536]{1,0:T(8,128)(2,1)} %reshape.168, bf16[1536,7168]{1,0:T(8,128)(2,1)} %all-gather.3.cloned.1.call-done), kind=kOutput, calls=%fused_computation.190 | convolution fusion | flops 6341787648 | bytes 31162368 | tf_op jit(solution)/shard_map/dot_general | solution.py:54
  221.5 95.7 %reduce-scatter.2.cloned.1.call-done = f32[288,3584]{1,0:T(8,128)} async-done(((f32[288,7168]{1,0:T(8,128)}), f32[288,3584]{1,0:T(8,128)}) %reduce-scatter.2.cloned.1.call-update) | async-done | bytes 4128784 | tf_op jit(solution)/shard_map/reduce_scatter | solution.py:55
  317.2 3.7 convert_element_type.43
  321.0 4.0 all_to_all.14
  324.9 5.4 all-to-all-start
  330.4 52.5 %all-to-all-done = bf16[8,36,3584]{2,1,0:T(8,128)(2,1)} async-done(((bf16[8,36,3584]{2,1,0:T(8,128)(2,1)}), bf16[8,36,3584]{2,1,0:T(8,128)(2,1)}, u32[]{:S(2)}, u32[]{:S(2)}) %all-to-all-start) | async-done | bytes 2064416 | tf_op jit(solution)/shard_map/all_to_all | solution.py:58
  382.8 4.0 reshape.184
  386.8 9.2 %scatter_fusion = bf16[576,3584]{1,0:T(8,128)(2,1)} fusion(bf16[576,3584]{1,0:T(8,128)(2,1)} %copy.23, s32[288]{0:T(512)S(1)} %fusion.7, bf16[288,3584]{1,0:T(8,128)(2,1)} %reshape.184), kind=kCustom, calls=%fused_computation.1 | custom fusion | bytes 6194304 | tf_op jit(solution)/shard_map/scatter | solution.py:60
  396.1 5.4 fusion.6
  401.5 3.9 all-reduce.2
  405.3 6.7 fusion.5
  412.0 10.0 %gather_fusion = bf16[288,3584]{1,0:T(8,128)(2,1)} fusion(bf16[576,3584]{1,0:T(8,128)(2,1)} %fusion.5, s32[1024]{0:T(1024)S(1)} %pad_clamp_fusion), kind=kCustom, calls=%fused_computation | custom fusion | bytes 4129920 | tf_op jit(solution)/shard_map/gather | solution.py:69
  422.1 4.0 convert_element_type.48
  426.1 58.7 %all_to_all.21 = bf16[8,36,3584]{2,1,0:T(8,128)(2,1)} all-to-all(bf16[8,36,3584]{2,1,0:T(8,128)(2,1)} %convert_element_type.48), channel_id=1, replica_groups=mesh['outer'=2,'sec'=8,'tp'=2] {'sec'}, dimensions={0} | all-to-all | bytes 4128768 | tf_op jit(solution)/shard_map/all_to_all | solution.py:70
  484.8 4.0 all_to_all.18
  488.9 54.2 %all-gather.5.cloned.1.call-done = bf16[288,7168]{1,0:T(8,128)(2,1)} async-done(((bf16[288,3584]{1,0:T(8,128)(2,1)}), bf16[288,7168]{1,0:T(8,128)(2,1)}) %all-gather.5.cloned.1.call-update) | async-done | bytes 4128784 | tf_op jit(solution)/shard_map/all_gather | solution.py:71
  543.1 13.2 %multiply_reduce_fusion.53 = (f32[1536]{0:T(1024)S(1)}, f32[288]{0:T(512)S(1)}, f32[288,1536]{1,0:T(8,128)}) fusion(f32[288]{0:T(512)S(1)} %reshape.171, f32[1536]{0:T(1024)S(1)} %copy-done.8, bf16[288,7168]{1,0:T(8,128)(2,1)} %all-gather.5.cloned.1.call-done, bf16[1536,7168]{1,0:T(8,128)(2,1)} %all-gather.3.cloned.1.call-done), kind=kOutput, calls=%fused_computation.120 | convolution fusion | flops 6343555072 | bytes 27932928 | tf_op jit(solution)/shard_map/dot_general | solution.py:72
  556.4 2.8 reshape.169
  559.1 3.4 multiply_reduce_fusion
  562.5 0.1 reduce_sum.529
  562.6 5.7 all-reduce.1
  568.3 9.6 %multiply_reduce_fusion.1 = (f32[1536]{0:T(1024)S(1)}, f32[1536]{0:T(1024)S(1)}, f32[1536]{0:T(1024)S(1)}, f32[1536]{0:T(1024)S(1)}, f32[1536]{0:T(1024)S(1)}, /...) fusion(f32[2,12,12,1536]{3,2,1,0:T(8,128)S(1)} %convert_multipl, ...), kind=kLoop, calls=%fused_computation.63 | loop fusion | flops 19436544 | bytes 7200384 | tf_op jit(solution)/shard_map/reduce_sum | solution.py:85
  577.9 6.3 multiply_reduce_fusion.19
  584.3 5.4 multiply_reduce_fusion.38
  590.4 4.8 stack.207
  595.3 56.8 %all-reduce.7.cloned.1.call-done = f32[51,1536]{1,0:T(8,128)} async-done(((f32[51,1536]{1,0:T(8,128)}), f32[51,1536]{1,0:T(8,128)}) %all-reduce.7.cloned.1.call-update) | async-done | bytes 313360 | tf_op jit(solution)/shard_map/psum | solution.py:91
  652.1 1.7 multiply_reduce_fusion.54
  653.8 4.4 psum.70
  658.9 1.7 broadcast_multiply_fusion.1
  660.6 5.5 fusion.2
  666.2 21.2 %all-reduce.9.cloned.1.call-done = f32[51,1536]{1,0:T(8,128)} async-done(((f32[51,1536]{1,0:T(8,128)}), f32[51,1536]{1,0:T(8,128)}) %all-reduce.9.cloned.1.call-update) | async-done | bytes 313360 | tf_op jit(solution)/shard_map/psum | solution.py:94
  687.4 1.0 broadcast_multiply_fusion
  688.4 0.6 slice_reduce_fusion
  689.0 0.8 reshape.170
  (89 shorter events, 0.9 us)
Async XLA Ops:
  7.2 201.2 %all-gather.3.cloned.1.call-start = ((), (), s32[]{:S(2)}) async-start(), calls=%async_computation.3 | async-start | bytes 24772608 | tf_op jit(solution)/shard_map/all_gather | solution.py:53
  11.6 0.7 copy-start.9
  11.6 1.0 copy-start.2
  11.6 2.6 copy-start
  11.7 305.6 %reduce-scatter.2.cloned.1.call-start = ((), (), s32[]{:S(2)}) async-start(), calls=%async_computation.4 | async-start | bytes 12386304 | tf_op jit(solution)/shard_map/reduce_scatter | solution.py:55
  46.1 0.6 copy-start.3
  46.1 0.6 copy-start.5
  324.9 5.4 copy-start.10
  324.9 57.9 %all-to-all-start = ((bf16[8,36,3584]{2,1,0:T(8,128)(2,1)}), bf16[8,36,3584]{2,1,0:T(8,128)(2,1)}, u32[]{:S(2)}, u32[]{:S(2)}) async-start(bf16[8,36,3584]{2,1,0:T(8,128)(2,1)} %all_to_all.14), calls=%async_computation.1 | async-start | bytes 4587520 | tf_op jit(solution)/shard_map/all_to_all | solution.py:58
  330.3 212.8 %all-gather.5.cloned.1.call-start = ((), (), s32[]{:S(2)}) async-start(), calls=%async_computation.5 | async-start | bytes 6193152 | tf_op jit(solution)/shard_map/all_gather | solution.py:71
  386.8 9.2 %copy-start.7 = (f32[3584]{0:T(1024)S(1)}, f32[3584]{0:T(1024)}, u32[]{:S(2)}) copy-start(f32[3584]{0:T(1024)} %param.18) | copy-start | bytes 43012
  484.8 58.4 %copy-start.8 = (f32[1536]{0:T(1024)S(1)}, f32[1536]{0:T(1024)}, u32[]{:S(2)}) copy-start(f32[1536]{0:T(1024)} %param.13) | copy-start | bytes 18436
  488.7 163.4 %all-reduce.7.cloned.1.call-start = ((), (), s32[]{:S(2)}) async-start(), calls=%async_computation.6 | async-start | bytes 688128 | tf_op jit(solution)/shard_map/psum | solution.py:91
  556.4 2.8 copy-start.4
  556.4 2.8 copy-start.6
  577.9 6.4 copy-start.1
  595.3 92.1 %all-reduce.9.cloned.1.call-start = ((), (), s32[]{:S(2)}) async-start(), calls=%async_computation.7 | async-start | bytes 688128 | tf_op jit(solution)/shard_map/psum | solution.py:94
Sparse Core Ops, SparseCore 0:
  11.8 196.5 all-gather.2
  221.6 95.5 reduce-scatter.1
  488.9 54.2 all-gather.4
  595.4 56.6 all-reduce.6
  660.8 26.5 all-reduce.8
where the time goes:
time: 698 us; the launch traced here: 696 us
  waiting for transfers between devices  438 us (63%)
  blocking collectives  80.6 us (12%)
  other arithmetic  78.1 us (11%)
  local copies, waits for them, and re-layouts  53.2 us (8%)
  matrix products  26.4 us (4%)
  between operations  15 us (2%)
    all_gather x1, waiting for transfers between devices, on_device(): whole_weight = lax.all_gather(projector, 'sec', axis=1, tiled=True)  157 us
    reduce_scatter x1, waiting for transfers between devices, on_device(): lax.psum_scatter(partial_value, 'tp', scatter_dimension=1, tiled=True)  95.7 us
    all_to_all x1, blocking collectives, on_device(): lax.all_to_all(picked, 'sec', split_axis=0, concat_axis=0, tiled=True)  58.7 us
    psum x1, waiting for transfers between devices, on_device(): pod_sum = lax.psum(local_delta, 'sec')  56.8 us
    all_gather x1, waiting for transfers between devices, on_device(): full_grad = lax.all_gather(returned, 'tp', axis=1, tiled=True)  54.2 us
    all_to_all x1, waiting for transfers between devices, on_device(): lax.all_to_all(visual, 'sec', split_axis=0, concat_axis=0, tiled=True)  52.5 us
    reduce_sum x1, other arithmetic, on_device(): jnp.sum(conv_out, axis=-1)  23.6 us
    reduce_sum x3, other arithmetic, on_device(): kernel_rows.append(jnp.sum(window * grad_conv, axis=(0, 1, 2)))  21.3 us
  transfers between devices with their start and end apart: 6, of which 6 were waited for; matrix products, arithmetic and copies ran while one was open for 5% of the time, Pallas kernels for 0%

commit v1 on v0

--- a/solution.py
+++ b/solution.py
@@ -50,12 +50,28 @@
         .astype(jnp.bfloat16)
         .reshape(rows_dev, half_ch)
     )
-    whole_weight = lax.all_gather(projector, "sec", axis=1, tiled=True)
-    partial_value = jnp.dot(features, whole_weight, preferred_element_type=jnp.float32)
-    visual = lax.psum_scatter(partial_value, "tp", scatter_dimension=1, tiled=True).astype(
-        jnp.bfloat16
-    )
-    arrived = lax.all_to_all(visual, "sec", split_axis=0, concat_axis=0, tiled=True)
+    tp_size = lax.axis_size("tp")
+    half_width = text_rows.shape[1]
+    mine = lax.axis_index("tp")
+    swap = [(i, (i + 1) % tp_size) for i in range(tp_size)]
+    gathered = lax.all_gather(projector, "sec", axis=0, tiled=False)
+    per_half = gathered.shape[0] // tp_size
+    own_weight = lax.dynamic_slice_in_dim(gathered, mine * per_half, per_half, axis=0)
+    far_weight = lax.dynamic_slice_in_dim(gathered, (1 - mine) * per_half, per_half, axis=0)
+    routed = lax.all_to_all(features, "sec", split_axis=0, concat_axis=0, tiled=True)
+
+    def project(rows, weight):
+        return jnp.concatenate(
+            [
+                jnp.dot(rows, weight[block], preferred_element_type=jnp.float32)
+                for block in range(per_half)
+            ],
+            axis=1,
+        )
+
+    sent = project(routed, far_weight).astype(jnp.bfloat16)
+    other = lax.ppermute(sent, "tp", swap)
+    arrived = (project(routed, own_weight) + other.astype(jnp.float32)).astype(jnp.bfloat16)
     positions = row_order[0, :rows_dev]
     merged = text_rows.at[positions].set(arrived)
     wide = merged.astype(jnp.float32)
@@ -67,9 +83,26 @@
     normed = (wide * inv_rms * seq_gain).astype(jnp.bfloat16)
     grad_seq = inv_rms * upstream - wide * (inv_rms * inv_rms * inv_rms) * along[:, None] / width
     picked = grad_seq[positions].astype(jnp.bfloat16)
-    returned = lax.all_to_all(picked, "sec", split_axis=0, concat_axis=0, tiled=True)
-    full_grad = lax.all_gather(returned, "tp", axis=1, tiled=True)
-    grad_rows = jnp.dot(full_grad, whole_weight.T, preferred_element_type=jnp.float32)
+    far_picked = lax.ppermute(picked, "tp", swap)
+
+    def project_back(rows, weight):
+        step = weight.shape[2]
+        total = jnp.zeros((rows.shape[0], half_ch), jnp.float32)
+        for block in range(per_half):
+            total = total + lax.dot_general(
+                rows[:, block * step : (block + 1) * step],
+                weight[block],
+                (((1,), (1,)), ((), ())),
+                preferred_element_type=jnp.float32,
+            )
+        return total
+
+    back = (project_back(picked, own_weight) + project_back(far_picked, far_weight)).astype(
+        jnp.bfloat16
+    )
+    grad_rows = lax.all_to_all(back, "sec", split_axis=0, concat_axis=0, tiled=True).astype(
+        jnp.float32
+    )
     masked_grad = grad_rows.reshape(masked.shape) * validity
     scaled = masked_grad * norm_gain
     first_sum, second_sum = lax.psum(

time: 698 us -> 561 us (0.80)
  waiting for transfers between devices: 438 us -> 335 us
  blocking collectives: 80.6 us -> 22.8 us
  matrix products: 26.4 us -> 46.6 us
  local copies, waits for them, and re-layouts: 53.2 us -> 38.2 us
  starting transfers between devices: 5.57 us -> 16.5 us
    reduce_scatter x1 -> x0, waiting for transfers between devices: 95.7 us -> none  [on_device(): lax.psum_scatter(partial_value, 'tp', scatter_dimension=1, tiled=True)]
    all_gather x2 -> x1, waiting for transfers between devices: 211 us -> 116 us  [on_device(): gathered = lax.all_gather(projector, 'sec', axis=0, tiled=False)]
    ppermute x0 -> x2, waiting for transfers between devices: none -> 65.3 us  [the longest x1 33.9 us: on_device(): other = lax.ppermute(sent, 'tp', swap)]
    all_to_all x1 -> x0, blocking collectives: 58.7 us -> none  [on_device(): lax.all_to_all(picked, 'sec', split_axis=0, concat_axis=0, tiled=True)]
    all_to_all x1 -> x2, waiting for transfers between devices: 52.5 us -> 78.3 us  [the longest x1 54.2 us: on_device(): lax.all_to_all(features, 'sec', split_axis=0, concat_axis=0, tiled=True)]
    dot_general x2 -> x16, matrix products: 26.4 us -> 46.6 us  [the longest x8 23.4 us: project_back(): lax.dot_general(rows[:, block * step:(block + 1) * step], weight[block],...]
    all_to_all x3, local copies, waits for them, and re-layouts: 11.9 us -> 3.31 us  [the longest x2 2.19 us: on_device(): lax.all_to_all(features, 'sec', split_axis=0, concat_axis=0, tiled=True)]
    all_to_all x1 -> x2, starting transfers between devices: 5.41 us -> 14 us  [the longest x1 7.01 us: on_device(): lax.all_to_all(back, 'sec', split_axis=0, concat_axis=0, tiled=True)]
  transfers between devices with their start and end apart: 6 -> 7, of which waited for: 6 -> 7; matrix products, arithmetic and copies ran while one was open for 5% -> 10% of each run, Pallas kernels for 0% -> 0%
where the time goes in v1:
time: 561 us; the launch traced here: 554 us
  waiting for transfers between devices  335 us (60%)
  other arithmetic  79.7 us (14%)
  matrix products  46.6 us (8%)
  local copies, waits for them, and re-layouts  38.2 us (7%)
  blocking collectives  22.8 us (4%)
  starting transfers between devices  16.5 us (3%)
  between operations  15.6 us (3%)
    all_gather x1, waiting for transfers between devices, on_device(): gathered = lax.all_gather(projector, 'sec', axis=0, tiled=False)  116 us
    all_to_all x1, waiting for transfers between devices, on_device(): lax.all_to_all(features, 'sec', split_axis=0, concat_axis=0, tiled=True)  54.2 us
    psum x1, waiting for transfers between devices, on_device(): pod_sum = lax.psum(local_delta, 'sec')  54 us
    ppermute x1, waiting for transfers between devices, on_device(): other = lax.ppermute(sent, 'tp', swap)  33.9 us
    ppermute x1, waiting for transfers between devices, on_device(): far_picked = lax.ppermute(picked, 'tp', swap)  31.4 us
    all_to_all x1, waiting for transfers between devices, on_device(): lax.all_to_all(back, 'sec', split_axis=0, concat_axis=0, tiled=True)  24.2 us
    reduce_sum x1, other arithmetic, on_device(): jnp.sum(conv_out, axis=-1)  23.6 us
    dot_general x8, matrix products, project_back(): lax.dot_general(rows[:, block * step:(block + 1) * step], weight[block],...  23.4 us
  transfers between devices with their start and end apart: 7, of which 7 were waited for; matrix products, arithmetic and copies ran while one was open for 10% of the time, Pallas kernels for 0%

profile of v1, /device:TPU:1, one launch (start us, length us, event | category | flops | bytes accessed | tf_op | source)
XLA Modules:
  0.0 554.1 jit_solution(14218790435124544517)
XLA Ops:
  7.2 4.4 copy.22
  14.4 23.6 %fusion.53 = (f32[2,12,12]{2,1,0:T(8,128)S(1)}, f32[2,12,12]{2,1,0:T(8,128)S(1)}, f32[2,12,12,1536]{3,2,1,0:T(8,128)}) fusion(f32[1536]{0:T(1024)S(1)} %get-tuple-element.110, f32[1536]{0:T(1024)S(1)} %get-tuple-element.111, f32[1536]{0:T(1024)S(1)} %get-tuple-element.64, f32[1536]{0:T(1024)S(1)} %get-tuple-element.65, f32[1536]{0:T(1024)S(1)} %get-tuple-element.66, ...), kind=kLoop, calls=%fused_computation.248 | loop fusion | flops 44236224 | bytes 3842304 | tf_op jit(solution)/shard_map/reduce_sum | solution.py:43
  38.1 8.0 %all-reduce.3 = (f32[2,12,12]{2,1,0:T(8,128)S(1)}, f32[2,12,12]{2,1,0:T(8,128)S(1)}) all-reduce(f32[2,12,12]{2,1,0:T(8,128)S(1)} %get-tuple-element.58, f32[2,12,12]{2,1,0:T(8,128)S(1)} %get-tuple-element.57), channel_id=1, replica_groups=mesh['outer'=2,'sec'=8,'tp'=2] {'tp'}, use_global_device_ids=true, to_apply=%region_3.4 | all-reduce | flops 576 | bytes 4608 | tf_op jit(solution)/shard_map/psum | solution.py:42
  46.7 3.5 multiply_convert_fusion
  51.3 6.9 %all-to-all-start = ((bf16[8,36,1536]{2,1,0:T(8,128)(2,1)}), bf16[8,36,1536]{2,1,0:T(8,128)(2,1)S(1)}, u32[]{:S(2)}, u32[]{:S(2)}) async-start(bf16[8,36,1536]{2,1,0:T(8,128)(2,1)} %all_to_all.14), calls=%async_computation | async-start | bytes 1966080 | tf_op jit(solution)/shard_map/all_to_all | solution.py:61
  58.2 54.2 %all-to-all-done = bf16[8,36,1536]{2,1,0:T(8,128)(2,1)S(1)} async-done(((bf16[8,36,1536]{2,1,0:T(8,128)(2,1)}), bf16[8,36,1536]{2,1,0:T(8,128)(2,1)S(1)}, u32[]{:S(2)}, u32[]{:S(2)}) %all-to-all-start) | async-done | bytes 884768 | tf_op jit(solution)/shard_map/all_to_all | solution.py:61
  113.5 115.9 %all-gather.3.cloned.1.call-done = bf16[12288,896]{1,0:T(8,128)(2,1)} async-done(((bf16[1536,896]{1,0:T(8,128)(2,1)}), bf16[12288,896]{1,0:T(8,128)(2,1)}) %all-gather.3.cloned.1.call-update) | async-done | bytes 22020112 | tf_op jit(solution)/shard_map/all_gather | solution.py:57
  229.3 3.2 fusion.27
  232.6 2.9 fusion.24
  235.4 2.9 fusion.25
  238.3 2.9 fusion.26
  241.2 1.5 pad_maximum_fusion
  243.9 2.9 fusion.13
  246.8 2.9 fusion.16
  249.6 2.9 fusion.15
  252.5 2.9 fusion.14
  255.3 33.9 %collective-permute-done = bf16[288,3584]{1,0:T(8,128)(2,1)} collective-permute-done((bf16[288,3584]{1,0:T(8,128)(2,1)}, bf16[288,3584]{1,0:T(8,128)(2,1)}, u32[]{:S(2)}, u32[]{:S(2)}) %collective-permute-start) | collective-permute-done | bytes 2064416 | tf_op jit(solution)/shard_map/ppermute | solution.py:73
  289.3 3.4 fusion.7
  292.7 9.2 %scatter_fusion = bf16[576,3584]{1,0:T(8,128)(2,1)} fusion(bf16[576,3584]{1,0:T(8,128)(2,1)} %copy.22, s32[288]{0:T(512)S(1)} %fusion.52, bf16[288,3584]{1,0:T(8,128)(2,1)} %fusion.7), kind=kCustom, calls=%fused_computation.1 | custom fusion | bytes 6194304 | tf_op jit(solution)/shard_map/scatter | solution.py:76
  301.9 5.4 fusion.6
  307.3 4.0 all-reduce.2
  311.4 6.7 %fusion.5 = bf16[576,3584]{1,0:T(8,128)(2,1)} fusion(bf16[576,3584]{1,0:T(8,128)(2,1)} %scatter_fusion, bf16[576,3584]{1,0:T(8,128)(2,1)} %param.19, f32[576]{0:T(1024)S(1)} %get-tuple-element.117, f32[576]{0:T(1024)S(1)} %get-tuple-element.124, f32[3584]{0:T(1024)S(1)} %copy-done.9, f32[576]{0:T(1024)S(1)} %get-tuple-element.125), kind=kLoop, calls=%fused_computation.59 | loop fusion | flops 18579456 | bytes 12407552 | tf_op jit(solution)/shard_map/sub | solution.py:84
  318.1 10.0 %gather_fusion = bf16[288,3584]{1,0:T(8,128)(2,1)} fusion(bf16[576,3584]{1,0:T(8,128)(2,1)} %fusion.5, s32[1024]{0:T(1024)S(1)} %pad_clamp_fusion), kind=kCustom, calls=%fused_computation | custom fusion | bytes 4129920 | tf_op jit(solution)/shard_map/gather | solution.py:85
  328.1 1.2 collective-permute-start.1
  329.3 3.0 fusion.12
  332.4 2.9 convolution_add_fusion.3
  335.3 2.9 convolution_add_fusion.2
  338.3 2.9 convolution_add_fusion.1
  341.2 31.4 %collective-permute-done.1 = bf16[288,3584]{1,0:T(8,128)(2,1)S(1)} collective-permute-done((bf16[288,3584]{1,0:T(8,128)(2,1)}, bf16[288,3584]{1,0:T(8,128)(2,1)S(1)}, u32[]{:S(2)}, u32[]{:S(2)}) %collective-permute-start.1) | collective-permute-done | bytes 2064416 | tf_op jit(solution)/shard_map/ppermute | solution.py:86
  372.6 2.9 fusion.22
  375.4 2.9 fusion.20
  378.3 2.9 fusion.18
  381.2 3.0 fusion.11
  385.4 7.0 %all-to-all-start.1 = ((bf16[8,36,1536]{2,1,0:T(8,128)(2,1)}), bf16[8,36,1536]{2,1,0:T(8,128)(2,1)S(1)}, u32[]{:S(2)}, u32[]{:S(2)}) async-start(bf16[8,36,1536]{2,1,0:T(8,128)(2,1)} %all_to_all.17), calls=%async_computation.1 | async-start | bytes 1966080 | tf_op jit(solution)/shard_map/all_to_all | solution.py:103
  392.5 24.2 %all-to-all-done.1 = bf16[8,36,1536]{2,1,0:T(8,128)(2,1)S(1)} async-done(((bf16[8,36,1536]{2,1,0:T(8,128)(2,1)}), bf16[8,36,1536]{2,1,0:T(8,128)(2,1)S(1)}, u32[]{:S(2)}, u32[]{:S(2)}) %all-to-all-start.1) | async-done | bytes 884768 | tf_op jit(solution)/shard_map/all_to_all | solution.py:103
  416.7 1.5 reshape.167
  418.2 3.4 multiply_reduce_fusion
  422.1 6.3 %all-reduce.1 = (f32[2,12,12]{2,1,0:T(8,128)S(1)}, f32[2,12,12]{2,1,0:T(8,128)S(1)}) all-reduce(f32[2,12,12]{2,1,0:T(8,128)S(1)} %get-tuple-element.5, f32[2,12,12]{2,1,0:T(8,128)S(1)} %reduce_sum.529), channel_id=1, replica_groups=mesh['outer'=2,'sec'=8,'tp'=2] {'tp'}, use_global_device_ids=true, to_apply=%region_12.13 | all-reduce | flops 576 | bytes 4608 | tf_op jit(solution)/shard_map/psum | solution.py:108
  428.5 9.6 %multiply_reduce_fusion.1 = (f32[1536]{0:T(1024)S(1)}, f32[1536]{0:T(1024)S(1)}, f32[1536]{0:T(1024)S(1)}, f32[1536]{0:T(1024)S(1)}, f32[1536]{0:T(1024)S(1)}, /...) fusion(f32[2,12,12,1536]{3,2,1,0:T(8,128)S(1)} %convert_multipl, ...), kind=kLoop, calls=%fused_computation.93 | loop fusion | flops 19436544 | bytes 7200384 | tf_op jit(solution)/shard_map/reduce_sum | solution.py:118
  438.1 5.4 multiply_reduce_fusion.38
  443.5 6.3 %multiply_reduce_fusion.19 = (f32[1536]{0:T(1024)S(1)}, f32[1536]{0:T(1024)S(1)}, f32[1536]{0:T(1024)S(1)}, f32[1536]{0:T(1024)S(1)}, f32[1536]{0:T(1024)S(1)}, ...) fusion(f32[2,12,12,1536]{3,2,1,0:T(8,128)S(1)} %get-tuple-eleme, ...), kind=kLoop, calls=%fused_computation.111 | loop fusion | flops 15897600 | bytes 3649536 | tf_op jit(solution)/shard_map/reduce_sum | solution.py:118
  450.6 4.8 stack.207
  455.5 54.0 %all-reduce.7.cloned.1.call-done = f32[51,1536]{1,0:T(8,128)} async-done(((f32[51,1536]{1,0:T(8,128)}), f32[51,1536]{1,0:T(8,128)}) %all-reduce.7.cloned.1.call-update) | async-done | bytes 313360 | tf_op jit(solution)/shard_map/psum | solution.py:124
  509.5 1.7 multiply_reduce_fusion.54
  511.2 4.4 psum.70
  516.3 1.7 broadcast_multiply_fusion.1
  518.0 5.5 fusion.2
  523.6 21.2 %all-reduce.9.cloned.1.call-done = f32[51,1536]{1,0:T(8,128)} async-done(((f32[51,1536]{1,0:T(8,128)}), f32[51,1536]{1,0:T(8,128)}) %all-reduce.9.cloned.1.call-update) | async-done | bytes 313360 | tf_op jit(solution)/shard_map/psum | solution.py:127
  (106 shorter events, 11.5 us)
Async XLA Ops:
  7.2 222.2 %all-gather.3.cloned.1.call-start = ((), (), s32[]{:S(2)}) async-start(), calls=%async_computation.4 | async-start | bytes 24772608 | tf_op jit(solution)/shard_map/all_gather | solution.py:57
  11.6 0.7 copy-start.11
  11.6 1.0 copy-start.4
  11.6 2.6 copy-start.1
  46.1 0.6 copy-start.5
  46.1 0.6 copy-start.7
  51.3 61.1 %all-to-all-start = ((bf16[8,36,1536]{2,1,0:T(8,128)(2,1)}), bf16[8,36,1536]{2,1,0:T(8,128)(2,1)S(1)}, u32[]{:S(2)}, u32[]{:S(2)}) async-start(bf16[8,36,1536]{2,1,0:T(8,128)(2,1)} %all_to_all.14), calls=%async_computation | async-start | bytes 1966080 | tf_op jit(solution)/shard_map/all_to_all | solution.py:61
  229.3 3.2 copy-start.3
  241.2 2.7 copy-start.12
  242.7 46.6 %collective-permute-start = (bf16[288,3584]{1,0:T(8,128)(2,1)}, bf16[288,3584]{1,0:T(8,128)(2,1)}, u32[]{:S(2)}, u32[]{:S(2)}) collective-permute-start(bf16[288,3584]{1,0:T(8,128)(2,1)} %pad_maximum_fusion), channel_id=1, source_target_pairs={{0,1},{1,0},{2,3},{3,2},{4,5},{5,4},{6,7},{7,6},{8,9},{9,8},{10,11... | collective-permute-start | bytes 6193160 | tf_op jit(solution)/shard_map/ppermute | solution.py:73
  292.7 9.2 %copy-start.9 = (f32[3584]{0:T(1024)S(1)}, f32[3584]{0:T(1024)}, u32[]{:S(2)}) copy-start(f32[3584]{0:T(1024)} %param.18) | copy-start | bytes 43012
  328.1 4.3 copy-start
  328.1 44.4 %collective-permute-start.1 = (bf16[288,3584]{1,0:T(8,128)(2,1)}, bf16[288,3584]{1,0:T(8,128)(2,1)S(1)}, u32[]{:S(2)}, u32[]{:S(2)}) collective-permute-start(bf16[288,3584]{1,0:T(8,128)(2,1)} %gather_fusion), channel_id=1, source_target_pairs={{0,1},{1,0},{2,3},{3,2},{4,5},{5,4},{6,7},{7,6},{8,9},{9,8},{10,11... | collective-permute-start | bytes 6193160 | tf_op jit(solution)/shard_map/ppermute | solution.py:86
  385.4 32.8 %copy-start.6 = (f32[2,12,12]{2,1,0:T(8,128)S(1)}, f32[2,12,12]{2,1,0:T(8,128)}, u32[]{:S(2)}) copy-start(f32[2,12,12]{2,1,0:T(8,128)} %copy-done.5) | copy-start | bytes 3460
  385.4 32.8 %copy-start.8 = (f32[2,12,12]{2,1,0:T(8,128)S(1)}, f32[2,12,12]{2,1,0:T(8,128)}, u32[]{:S(2)}) copy-start(f32[2,12,12]{2,1,0:T(8,128)} %copy-done.7) | copy-start | bytes 3460
  385.4 32.8 %copy-start.10 = (f32[1536]{0:T(1024)S(1)}, f32[1536]{0:T(1024)}, u32[]{:S(2)}) copy-start(f32[1536]{0:T(1024)} %param.13) | copy-start | bytes 18436
  385.4 31.3 %all-to-all-start.1 = ((bf16[8,36,1536]{2,1,0:T(8,128)(2,1)}), bf16[8,36,1536]{2,1,0:T(8,128)(2,1)S(1)}, u32[]{:S(2)}, u32[]{:S(2)}) async-start(bf16[8,36,1536]{2,1,0:T(8,128)(2,1)} %all_to_all.17), calls=%async_computation.1 | async-start | bytes 1966080 | tf_op jit(solution)/shard_map/all_to_all | solution.py:103
  392.4 117.1 %all-reduce.7.cloned.1.call-start = ((), (), s32[]{:S(2)}) async-start(), calls=%async_computation.2 | async-start | bytes 688128 | tf_op jit(solution)/shard_map/psum | solution.py:124
  428.5 9.6 %copy-start.2 = (bf16[2,12,12,1536]{3,0,2,1:T(2,128)(2,1)S(1)}, bf16[2,12,12,1536]{3,0,2,1:T(2,128)(2,1)}, u32[]{:S(2)}) copy-start(bf16[2,12,12,1536]{3,0,2,1:T(2,128)(2,1)} %param.10) | copy-start | bytes 2654212
  455.4 89.3 %all-reduce.9.cloned.1.call-start = ((), (), s32[]{:S(2)}) async-start(), calls=%async_computation.3 | async-start | bytes 688128 | tf_op jit(solution)/shard_map/psum | solution.py:127
Sparse Core Ops, SparseCore 0:
  11.8 217.5 all-gather.2
  455.6 53.8 all-reduce.6
  518.2 26.5 all-reduce.8

commit v2 on v1

--- a/solution.py
+++ b/solution.py
@@ -1,7 +1,288 @@
 import jax
 import jax.numpy as jnp
 from jax import lax
+from jax.experimental import pallas as pl
+from jax.experimental.pallas import tpu as pltpu
 from jax.sharding import PartitionSpec as P
+import functools
+
+MESH = pl.DeviceIdType.MESH
+
+
+def gather_kernel(
+    n_sec, pieces, own_ref, left_ref, right_ref, tie_ref, out_ref,
+    near_sem, z_send, z_recv, x_send, x_recv, c_send, c_recv, cx_send, cx_recv,
+):
+    chips = n_sec // 2
+    pod = lax.axis_index("outer")
+    sec = lax.axis_index("sec")
+    tp = lax.axis_index("tp")
+    core = sec % 2
+    chip = sec // 2
+    half = own_ref.shape[0] // 2
+    rows = half // pieces
+    right_ok = chip + 1 < chips
+    left_ok = chip >= 1
+
+    barrier = pltpu.get_barrier_semaphore()
+
+    def greet(to_pod, to_sec):
+        pl.semaphore_signal(barrier, inc=1, device_id=(to_pod, to_sec, tp), device_id_type=MESH)
+
+    greet(1 - pod, sec)
+    greet(pod, 2 * chip + 1 - core)
+    pl.when(right_ok)(lambda: greet(pod, sec + 2))
+    pl.when(left_ok)(lambda: greet(pod, sec - 2))
+    pl.semaphore_wait(barrier, 2 + right_ok.astype(jnp.int32) + left_ok.astype(jnp.int32))
+
+    def span(part, k):
+        return pl.ds(pl.multiple_of(part * half + k * rows, rows), rows)
+
+    def place(unit, on_core, part, k):
+        return out_ref.at[2 * unit + on_core, span(part, k)]
+
+    def source(unit, side, d, k):
+        if d > 1:
+            return place(unit, core, pod, k)
+        ref = left_ref if side == 0 else right_ref
+        return ref.at[pl.ds(k * rows, rows)]
+
+    def remote(src, dst, send, recv, to_pod, to_sec):
+        return pltpu.make_async_remote_copy(
+            src_ref=src, dst_ref=dst, send_sem=send, recv_sem=recv,
+            device_id=(to_pod, to_sec, tp), device_id_type=MESH,
+        )
+
+    def z_copy(unit, side, d, k):
+        return remote(
+            source(unit, side, d, k), place(unit, core, pod, k),
+            z_send.at[unit, k], z_recv.at[unit, k],
+            pod, sec + 2 if side == 0 else sec - 2,
+        )
+
+    def x_copy(unit, side, d, k):
+        return remote(
+            source(unit, side, d, k), place(unit, core, pod, k),
+            x_send.at[unit, k], x_recv.at[unit, k], 1 - pod, sec,
+        )
+
+    def c_copy(unit, side, d, k):
+        return remote(
+            source(unit, side, d, k), place(unit, core, pod, k),
+            c_send.at[unit, k], c_recv.at[unit, k], pod, 2 * chip + 1 - core,
+        )
+
+    def cx_copy(unit, k):
+        return remote(
+            place(unit, core, 1 - pod, k), place(unit, core, 1 - pod, k),
+            cx_send.at[unit, k], cx_recv.at[unit, k], pod, 2 * chip + 1 - core,
+        )
+
+    own_core = remote(
+        own_ref, out_ref.at[sec], c_send.at[chip, 0], c_recv.at[chip, 0],
+        pod, 2 * chip + 1 - core,
+    )
+    own_local = pltpu.make_async_copy(own_ref, out_ref.at[sec], near_sem.at[0])
+
+    def near_copy(side):
+        unit = chip - 1 if side == 0 else chip + 1
+        ref = left_ref if side == 0 else right_ref
+        return pltpu.make_async_copy(
+            ref,
+            out_ref.at[2 * unit + core, pl.ds(pl.multiple_of(pod * half, half), half)],
+            near_sem.at[1 + side],
+        )
+
+    def unit_of(side, d):
+        unit = chip - d if side == 0 else chip + d
+        valid = unit >= 0 if side == 0 else unit < chips
+        onward = jnp.logical_and(valid, right_ok if side == 0 else left_ok)
+        return unit, valid, onward
+
+    def take_x(d, k):
+        for side in (0, 1):
+            unit, valid, _ = unit_of(side, d)
+
+            @pl.when(valid)
+            def _():
+                x_copy(unit, side, d, k).wait_recv()
+                cx_copy(unit, k).start()
+
+    for d in range(1, chips):
+        for k in range(pieces):
+            for side in (0, 1):
+                unit, valid, onward = unit_of(side, d)
+
+                @pl.when(valid)
+                def _():
+                    if d > 1:
+                        z_copy(unit, side, d, k).wait_recv()
+
+                @pl.when(onward)
+                def _():
+                    z_copy(unit, side, d, k).start()
+
+                @pl.when(valid)
+                def _():
+                    x_copy(unit, side, d, k).start()
+                    c_copy(unit, side, d, k).start()
+
+            if d > 1:
+                take_x(d - 1, k)
+        if d == 1:
+            own_core.start()
+            own_local.start()
+            for side in (0, 1):
+                pl.when(unit_of(side, 1)[1])(lambda side=side: near_copy(side).start())
+    for k in range(pieces):
+        take_x(chips - 1, k)
+
+    own_local.wait()
+    own_core.wait()
+    for side in (0, 1):
+        pl.when(unit_of(side, 1)[1])(lambda side=side: near_copy(side).wait())
+    for d in range(1, chips):
+        for k in range(pieces):
+            for side in (0, 1):
+                unit, valid, onward = unit_of(side, d)
+
+                @pl.when(onward)
+                def _():
+                    z_copy(unit, side, d, k).wait_send()
+
+                @pl.when(valid)
+                def _():
+                    x_copy(unit, side, d, k).wait_send()
+                    c_copy(unit, side, d, k).wait()
+                    cx_copy(unit, k).wait()
+
+
+def gather_blocks(projector, left, right, tie):
+    n_sec = lax.axis_size("sec")
+    chips = n_sec // 2
+    pieces = 4 if chips <= 4 else 1
+    pair = pltpu.SemaphoreType.DMA((chips, pieces))
+    return pl.pallas_call(
+        functools.partial(gather_kernel, n_sec, pieces),
+        out_shape=jax.ShapeDtypeStruct((n_sec,) + projector.shape, projector.dtype),
+        in_specs=[pl.BlockSpec(memory_space=pl.ANY)] * 4,
+        out_specs=pl.BlockSpec(memory_space=pl.ANY),
+        scratch_shapes=[pltpu.SemaphoreType.DMA((3,))] + [pair] * 8,
+        compiler_params=pltpu.CompilerParams(collective_id=0, has_side_effects=True),
+        cost_estimate=pl.CostEstimate(
+            flops=0, bytes_accessed=200_000_000, transcendentals=0
+        ),
+    )(projector, left, right, tie)
+
+
+def clip_kernel(
+    n_sec, n_tp, entries, delta_ref, out_ref,
+    parts, norm_own, norms, scaled, far, part_send, part_recv,
+    norm_send, norm_recv, far_sem, all_send, all_recv,
+):
+    pod = lax.axis_index("outer")
+    sec = lax.axis_index("sec")
+    tp = lax.axis_index("tp")
+    barrier = pltpu.get_barrier_semaphore()
+    peers = n_sec * n_tp
+    me = tp * n_sec + sec
+
+    def peer(j):
+        other = lax.rem(me + j, peers)
+        return (pod, other % n_sec, other // n_sec)
+
+    for j in range(1, peers):
+        pl.semaphore_signal(barrier, inc=1, device_id=peer(j), device_id_type=MESH)
+    pl.semaphore_signal(barrier, inc=1, device_id=(1 - pod, sec, tp), device_id_type=MESH)
+    pl.semaphore_wait(barrier, peers)
+
+    def part_copy(j):
+        to = lax.rem(sec + j, n_sec)
+        return pltpu.make_async_remote_copy(
+            src_ref=delta_ref.at[to], dst_ref=parts.at[j - 1],
+            send_sem=part_send.at[j - 1], recv_sem=part_recv.at[j - 1],
+            device_id=(pod, to, tp), device_id_type=MESH,
+        )
+
+    def norm_copy(j):
+        return pltpu.make_async_remote_copy(
+            src_ref=norm_own, dst_ref=norms.at[j - 1],
+            send_sem=norm_send.at[j - 1], recv_sem=norm_recv.at[j - 1],
+            device_id=peer(j), device_id_type=MESH,
+        )
+
+    def all_copy(j):
+        to = lax.rem(sec + j, n_sec)
+        return pltpu.make_async_remote_copy(
+            src_ref=out_ref.at[sec], dst_ref=out_ref.at[sec],
+            send_sem=all_send.at[j - 1], recv_sem=all_recv.at[j - 1],
+            device_id=(pod, to, tp), device_id_type=MESH,
+        )
+
+    for j in range(1, n_sec):
+        part_copy(j).start()
+    total = delta_ref[sec]
+    for j in range(1, n_sec):
+        part_copy(j).wait_recv()
+        total = total + parts[j - 1]
+    norm_own[...] = jnp.broadcast_to(jnp.sum(total * total, keepdims=True), norm_own.shape)
+    for j in range(1, peers):
+        norm_copy(j).start()
+    square = norm_own[...]
+    for j in range(1, peers):
+        norm_copy(j).wait_recv()
+        square = square + norms[j - 1]
+    factor = jnp.minimum(1.0, 1.0 / jnp.sqrt(square / entries + 1e-06))
+    scaled[...] = total * factor[0:1, 0:1]
+    across = pltpu.make_async_remote_copy(
+        src_ref=scaled, dst_ref=far, send_sem=far_sem.at[0], recv_sem=far_sem.at[1],
+        device_id=(1 - pod, sec, tp), device_id_type=MESH,
+    )
+    across.start()
+    across.wait()
+    out_ref[sec] = (scaled[...] + far[...]) * 0.5
+    for j in range(1, n_sec):
+        all_copy(j).start()
+    for j in range(1, n_sec):
+        all_copy(j).wait()
+        part_copy(j).wait_send()
+    for j in range(1, peers):
+        norm_copy(j).wait_send()
+
+
+def clipped_mean(local_delta):
+    n_sec = lax.axis_size("sec")
+    n_tp = lax.axis_size("tp")
+    rows, width = local_delta.shape
+    share = -(-rows // n_sec)
+    stacked = jnp.pad(local_delta, ((0, share * n_sec - rows), (0, 0)))
+    stacked = stacked.reshape(n_sec, share, width)
+    shard = (share, width)
+    dma = pltpu.SemaphoreType.DMA
+    average = pl.pallas_call(
+        functools.partial(clip_kernel, n_sec, n_tp, rows * width * n_tp),
+        out_shape=jax.ShapeDtypeStruct(stacked.shape, jnp.float32),
+        in_specs=[pl.BlockSpec(memory_space=pltpu.VMEM)],
+        out_specs=pl.BlockSpec(memory_space=pltpu.VMEM),
+        scratch_shapes=[
+            pltpu.VMEM((n_sec - 1,) + shard, jnp.float32),
+            pltpu.VMEM((8, 128), jnp.float32),
+            pltpu.VMEM((n_sec * n_tp - 1, 8, 128), jnp.float32),
+            pltpu.VMEM(shard, jnp.float32),
+            pltpu.VMEM(shard, jnp.float32),
+            dma((n_sec - 1,)),
+            dma((n_sec - 1,)),
+            dma((n_sec * n_tp - 1,)),
+            dma((n_sec * n_tp - 1,)),
+            dma((2,)),
+            dma((n_sec - 1,)),
+            dma((n_sec - 1,)),
+        ],
+        compiler_params=pltpu.CompilerParams(
+            collective_id=1, has_side_effects=True, vmem_limit_bytes=24 * 1024 * 1024
+        ),
+    )(stacked)
+    return average.reshape(n_sec * share, width)[:rows]
 
 
 def shape_mask(tile_shape, grid):
@@ -28,6 +309,13 @@
     channels = half_ch * lax.axis_size("tp")
     rows_dev = tile_maps.shape[0] * grid * grid
     width = text_rows.shape[1] * lax.axis_size("tp")
+    n_sec = lax.axis_size("sec")
+    half_rows = projector.shape[0] // 2
+    first_half = lax.dynamic_slice_in_dim(
+        projector, lax.axis_index("outer") * half_rows, half_rows, axis=0
+    )
+    from_left = lax.ppermute(first_half, "sec", [(i, i + 2) for i in range(n_sec - 2)])
+    from_right = lax.ppermute(first_half, "sec", [(i + 2, i) for i in range(n_sec - 2)])
     validity = shape_mask(tile_shape, grid)[..., None]
     masked = tile_maps.astype(jnp.float32) * validity
     padded = jnp.pad(masked, ((0, 0), (3, 3), (3, 3), (0, 0)))
@@ -54,7 +342,7 @@
     half_width = text_rows.shape[1]
     mine = lax.axis_index("tp")
     swap = [(i, (i + 1) % tp_size) for i in range(tp_size)]
-    gathered = lax.all_gather(projector, "sec", axis=0, tiled=False)
+    gathered = gather_blocks(projector, from_left, from_right, features)
     per_half = gathered.shape[0] // tp_size
     own_weight = lax.dynamic_slice_in_dim(gathered, mine * per_half, per_half, axis=0)
     far_weight = lax.dynamic_slice_in_dim(gathered, (1 - mine) * per_half, per_half, axis=0)
@@ -119,12 +407,7 @@
     gain_grad = jnp.sum(masked_grad * normal, axis=(0, 1, 2))
     bias_grad = jnp.sum(masked_grad, axis=(0, 1, 2))
     local_delta = jnp.stack(kernel_rows + [gain_grad, bias_grad], axis=0)
-    pods = lax.axis_size("outer")
-    entries = 51 * channels
-    pod_sum = lax.psum(local_delta, "sec")
-    norm_sq = lax.psum(jnp.sum(pod_sum * pod_sum), "tp")
-    factor = jnp.minimum(1.0, 1.0 / jnp.sqrt(norm_sq / entries + 1e-06))
-    average = lax.psum(pod_sum * factor, "outer") / pods
+    average = clipped_mean(local_delta)
     return (normed, average[:49].reshape(7, 7, half_ch), average[49], average[50])
 
 

time: 561 us -> 535 us (0.954)
  waiting for transfers between devices: 335 us -> 125 us
  Pallas kernels: 0 us -> 165 us
  starting transfers between devices: 16.5 us -> 63.2 us
  between operations: 15.6 us -> 1.89 us
  other arithmetic: 79.7 us -> 73.7 us
  blocking collectives: 22.8 us -> 17 us
    pallas_call x0 -> x2, Pallas kernels: none -> 165 us  [the longest x1 134 us: gather_blocks(): pl.pallas_call(functools.partial(gather_kernel, n_sec, pieces), out_shape...]
    all_gather x1 -> x0, waiting for transfers between devices: 116 us -> none  [on_device(): gathered = lax.all_gather(projector, 'sec', axis=0, tiled=False)]
    psum x2 -> x0, waiting for transfers between devices: 75.2 us -> none  [the longest x1 54 us: on_device(): pod_sum = lax.psum(local_delta, 'sec')]
    all_to_all x1, waiting for transfers between devices: 54.2 us -> 0.01 us  [on_device(): lax.all_to_all(features, 'sec', split_axis=0, concat_axis=0, tiled=True)]
    all_to_all x1, starting transfers between devices: 7.01 us -> 49.5 us  [on_device(): lax.all_to_all(back, 'sec', split_axis=0, concat_axis=0, tiled=True)]
    ppermute x0 -> x2, waiting for transfers between devices: none -> 38.1 us  [the longest x1 36.6 us: on_device(): lax.ppermute(first_half, 'sec', [(i, i + 2) for i in range(n_sec - 2)])]
    ppermute x0 -> x2, starting transfers between devices: none -> 5.67 us  [the longest x1 4.39 us: on_device(): lax.ppermute(first_half, 'sec', [(i, i + 2) for i in range(n_sec - 2)])]
  transfers between devices with their start and end apart: 7 -> 6, of which waited for: 7 -> 5; matrix products, arithmetic and copies ran while one was open for 10% -> 6% of each run, Pallas kernels for 0% -> 25%
where the time goes in v2:
time: 535 us; the launch traced here: 528 us
  Pallas kernels  165 us (31%)
  waiting for transfers between devices  125 us (23%)
  other arithmetic  73.7 us (14%)
  starting transfers between devices  63.2 us (12%)
  matrix products  46.4 us (9%)
  local copies, waits for them, and re-layouts  36.7 us (7%)
  blocking collectives  17 us (3%)
    pallas_call x1, Pallas kernels, gather_blocks(): pl.pallas_call(functools.partial(gather_kernel, n_sec, pieces), out_shape...  134 us
    all_to_all x1, starting transfers between devices, on_device(): lax.all_to_all(back, 'sec', split_axis=0, concat_axis=0, tiled=True)  49.5 us
    ppermute x1, waiting for transfers between devices, on_device(): lax.ppermute(first_half, 'sec', [(i, i + 2) for i in range(n_sec - 2)])  36.6 us
    ppermute x1, waiting for transfers between devices, on_device(): far_picked = lax.ppermute(picked, 'tp', swap)  34.2 us
    ppermute x1, waiting for transfers between devices, on_device(): other = lax.ppermute(sent, 'tp', swap)  33.9 us
    pallas_call x1, Pallas kernels, clipped_mean(): pl.pallas_call(functools.partial(clip_kernel, n_sec, n_tp, rows * width *...  30.5 us
    dot_general x8, matrix products, project_back(): lax.dot_general(rows[:, block * step:(block + 1) * step], weight[block],...  23.5 us
    dot_general x8, matrix products, project(): jnp.dot(rows, weight[block], preferred_element_type=jnp.float32)  22.8 us
  transfers between devices with their start and end apart: 6, of which 5 were waited for; matrix products, arithmetic and copies ran while one was open for 6% of the time, Pallas kernels for 25%

profile of v2, /device:TPU:1, one launch (start us, length us, event | category | flops | bytes accessed | tf_op | source)
XLA Modules:
  0.0 528.5 jit_solution(4831297223410546758)
XLA Ops:
  0.7 4.5 copy.21
  6.6 22.2 %fusion.57 = (f32[2,12,12]{2,1,0:T(8,128)S(1)}, f32[2,12,12]{2,1,0:T(8,128)S(1)}, f32[2,12,12,1536]{3,2,1,0:T(8,128)}) fusion(f32[1536]{0:T(1024)S(1)} %get-tuple-element.110, f32[1536]{0:T(1024)S(1)} %get-tuple-element.111, f32[1536]{0:T(1024)S(1)} %get-tuple-element.64, f32[1536]{0:T(1024)S(1)} %get-tuple-element.65, f32[1536]{0:T(1024)S(1)} %get-tuple-element.66, ...), kind=kLoop, calls=%fused_computation.248 | loop fusion | flops 44236224 | bytes 3842304 | tf_op jit(solution)/shard_map/reduce_sum | solution.py:331
  28.8 7.2 %all-reduce.4 = (f32[2,12,12]{2,1,0:T(8,128)S(1)}, f32[2,12,12]{2,1,0:T(8,128)S(1)}) all-reduce(f32[2,12,12]{2,1,0:T(8,128)S(1)} %get-tuple-element.58, f32[2,12,12]{2,1,0:T(8,128)S(1)} %get-tuple-element.57), channel_id=1, replica_groups=mesh['outer'=2,'sec'=8,'tp'=2] {'tp'}, use_global_device_ids=true, to_apply=%region_3.4 | all-reduce | flops 576 | bytes 4608 | tf_op jit(solution)/shard_map/psum | solution.py:330
  36.6 3.4 multiply_convert_fusion
  40.0 1.1 all_to_all.14
  41.2 7.6 %all-to-all-start = ((bf16[8,36,1536]{2,1,0:T(8,128)(2,1)}), bf16[8,36,1536]{2,1,0:T(8,128)(2,1)}, u32[]{:S(2)}, u32[]{:S(2)}) async-start(bf16[8,36,1536]{2,1,0:T(8,128)(2,1)} %all_to_all.14), calls=%async_computation | async-start | bytes 1966080 | tf_op jit(solution)/shard_map/all_to_all | solution.py:349
  48.8 2.5 constant_dynamic-slice_fusion
  51.3 4.4 collective-permute-start
  55.7 1.3 collective-permute-start.1
  58.1 36.6 %collective-permute-done.left_ref = bf16[768,896]{1,0:T(8,128)(2,1)} collective-permute-done((bf16[768,896]{1,0:T(8,128)(2,1)}, bf16[768,896]{1,0:T(8,128)(2,1)}, u32[]{:S(2)}, u32[]{:S(2)}) %collective-permute-start) | collective-permute-done | bytes 1376288 | tf_op jit(solution)/shard_map/ppermute | solution.py:317
  94.7 1.5 collective-permute-done.1.right_ref
  96.2 134.3 %shard_map.129 = bf16[8,1536,896]{2,1,0:T(8,128)(2,1)} custom-call(bf16[1536,896]{1,0:T(8,128)(2,1)} %own_ref.1, bf16[768,896]{1,0:T(8,128)(2,1)} %collective-permute-done.left_ref, bf16[768,896]{1,0:T(8,128)(2,1)} %collective-permute-done.1.right_ref, bf16[288,1536]{1,0:T(8,128)(2,1)} %reshape.174.tie_ref), custom_call_target="tpu_custom_call" | custom-call | bytes 200000000 | tf_op jit(solution)/shard_map/pallas_call | solution.py:165
  230.5 1.3 all_to_all.16
  231.9 2.9 fusion.31
  234.7 2.9 fusion.28
  237.6 2.9 fusion.29
  240.5 2.9 fusion.30
  243.3 1.5 pad_maximum_fusion
  245.1 2.9 fusion.14
  247.9 2.9 fusion.20
  250.8 2.9 fusion.18
  253.6 2.9 fusion.16
  256.5 33.9 %collective-permute-done.2 = bf16[288,3584]{1,0:T(8,128)(2,1)} collective-permute-done((bf16[288,3584]{1,0:T(8,128)(2,1)}, bf16[288,3584]{1,0:T(8,128)(2,1)}, u32[]{:S(2)}, u32[]{:S(2)}) %collective-permute-start.2) | collective-permute-done | bytes 2064416 | tf_op jit(solution)/shard_map/ppermute | solution.py:361
  290.4 3.4 fusion.7
  293.7 9.2 %scatter_fusion = bf16[576,3584]{1,0:T(8,128)(2,1)} fusion(bf16[576,3584]{1,0:T(8,128)(2,1)} %copy.21, s32[288]{0:T(512)S(1)} %fusion.56, bf16[288,3584]{1,0:T(8,128)(2,1)} %fusion.7), kind=kCustom, calls=%fused_computation.1 | custom fusion | bytes 6194304 | tf_op jit(solution)/shard_map/scatter | solution.py:364
  303.0 5.4 %fusion.6 = (f32[576]{0:T(1024)S(1)}, f32[576]{0:T(1024)S(1)}) fusion(bf16[576,3584]{1,0:T(8,128)(2,1)} %scatter_fusion, bf16[576,3584]{1,0:T(8,128)(2,1)} %param.19, f32[3584]{0:T(1024)S(1)} %copy-done.8), kind=kLoop, calls=%fused_computation.60 | loop fusion | flops 14449536 | bytes 8276480 | tf_op jit(solution)/shard_map/reduce_sum | solution.py:368
  308.4 4.0 all-reduce.3
  312.4 6.7 %fusion.5 = bf16[576,3584]{1,0:T(8,128)(2,1)} fusion(bf16[576,3584]{1,0:T(8,128)(2,1)} %scatter_fusion, bf16[576,3584]{1,0:T(8,128)(2,1)} %param.19, f32[576]{0:T(1024)S(1)} %get-tuple-element.117, f32[576]{0:T(1024)S(1)} %get-tuple-element.124, f32[3584]{0:T(1024)S(1)} %copy-done.8, f32[576]{0:T(1024)S(1)} %get-tuple-element.125), kind=kLoop, calls=%fused_computation.59 | loop fusion | flops 18579456 | bytes 12407552 | tf_op jit(solution)/shard_map/sub | solution.py:372
  319.1 10.0 %gather_fusion = bf16[288,3584]{1,0:T(8,128)(2,1)} fusion(bf16[576,3584]{1,0:T(8,128)(2,1)} %fusion.5, s32[1024]{0:T(1024)S(1)} %pad_clamp_fusion), kind=kCustom, calls=%fused_computation | custom fusion | bytes 4129920 | tf_op jit(solution)/shard_map/gather | solution.py:373
  329.4 3.2 fusion.19
  332.6 2.9 fusion.17
  335.5 2.9 fusion.15
  338.4 34.2 %collective-permute-done.3 = bf16[288,3584]{1,0:T(8,128)(2,1)S(1)} collective-permute-done((bf16[288,3584]{1,0:T(8,128)(2,1)}, bf16[288,3584]{1,0:T(8,128)(2,1)S(1)}, u32[]{:S(2)}, u32[]{:S(2)}) %collective-permute-start.3) | collective-permute-done | bytes 2064416 | tf_op jit(solution)/shard_map/ppermute | solution.py:374
  372.6 2.9 fusion.26
  375.4 2.9 fusion.24
  378.3 2.9 fusion.22
  381.2 2.9 fusion.10
  384.2 3.0 fusion.13
  388.3 49.5 %all-to-all-start.1 = ((bf16[8,36,1536]{2,1,0:T(8,128)(2,1)}), bf16[8,36,1536]{2,1,0:T(8,128)(2,1)S(1)}, u32[]{:S(2)}, u32[]{:S(2)}) async-start(bf16[8,36,1536]{2,1,0:T(8,128)(2,1)} %all_to_all.17), calls=%async_computation.1 | async-start | bytes 1966080 | tf_op jit(solution)/shard_map/all_to_all | solution.py:391
  437.9 5.5 %fusion.2 = bf16[576,3584]{1,0:T(8,128)(2,1)} fusion(bf16[576,3584]{1,0:T(8,128)(2,1)} %scatter_fusion, f32[3584]{0:T(1024)S(1)} %copy-done.8, f32[576]{0:T(1024)S(1)} %get-tuple-element.125), kind=kLoop, calls=%fused_computation.56 | loop fusion | flops 8257536 | bytes 8274176 | tf_op jit(solution)/shard_map/convert_element_type | solution.py:371
  443.4 18.7 %all-to-all-done.1 = bf16[8,36,1536]{2,1,0:T(8,128)(2,1)S(1)} async-done(((bf16[8,36,1536]{2,1,0:T(8,128)(2,1)}), bf16[8,36,1536]{2,1,0:T(8,128)(2,1)S(1)}, u32[]{:S(2)}, u32[]{:S(2)}) %all-to-all-start.1) | async-done | bytes 884768 | tf_op jit(solution)/shard_map/all_to_all | solution.py:391
  462.1 1.5 reshape.177
  463.6 3.4 multiply_reduce_fusion
  467.5 5.7 %all-reduce.2 = (f32[2,12,12]{2,1,0:T(8,128)S(1)}, f32[2,12,12]{2,1,0:T(8,128)S(1)}) all-reduce(f32[2,12,12]{2,1,0:T(8,128)S(1)} %get-tuple-element.5, f32[2,12,12]{2,1,0:T(8,128)S(1)} %reduce_sum.520), channel_id=1, replica_groups=mesh['outer'=2,'sec'=8,'tp'=2] {'tp'}, use_global_device_ids=true, to_apply=%region_12.13 | all-reduce | flops 576 | bytes 4608 | tf_op jit(solution)/shard_map/psum | solution.py:396
  473.3 9.6 %multiply_reduce_fusion.1 = (f32[1536]{0:T(1024)S(1)}, f32[1536]{0:T(1024)S(1)}, f32[1536]{0:T(1024)S(1)}, f32[1536]{0:T(1024)S(1)}, f32[1536]{0:T(1024)S(1)}, /...) fusion(f32[2,12,12,1536]{3,2,1,0:T(8,128)S(1)} %convert_multipl, ...), kind=kLoop, calls=%fused_computation.95 | loop fusion | flops 19436544 | bytes 7200384 | tf_op jit(solution)/shard_map/reduce_sum | solution.py:406
  482.9 5.4 %multiply_reduce_fusion.38 = (f32[1536]{0:T(1024)S(1)}, f32[1536]{0:T(1024)S(1)}, f32[1536]{0:T(1024)S(1)}, f32[1536]{0:T(1024)S(1)}, f32[1536]{0:T(1024)S(1)}, ...) fusion(f32[2,12,12,1536]{3,2,1,0:T(8,128)S(1)} %get-tuple-eleme, ...), kind=kLoop, calls=%fused_computation.132 | loop fusion | flops 12366336 | bytes 4504704 | tf_op jit(solution)/shard_map/reduce_sum | solution.py:406
  488.3 6.3 %multiply_reduce_fusion.19 = (f32[1536]{0:T(1024)S(1)}, f32[1536]{0:T(1024)S(1)}, f32[1536]{0:T(1024)S(1)}, f32[1536]{0:T(1024)S(1)}, f32[1536]{0:T(1024)S(1)}, ...) fusion(f32[2,12,12,1536]{3,2,1,0:T(8,128)S(1)} %get-tuple-eleme, ...), kind=kLoop, calls=%fused_computation.113 | loop fusion | flops 15897600 | bytes 3649536 | tf_op jit(solution)/shard_map/reduce_sum | solution.py:406
  496.0 30.5 %shard_map.130 = f32[8,7,1536]{2,1,0:T(8,128)S(1)} custom-call(f32[8,7,1536]{2,1,0:T(8,128)S(1)} %reshape.175.delta_ref), custom_call_target="tpu_custom_call" | custom-call | tf_op jit(solution)/shard_map/pallas_call | solution.py:262
  (102 shorter events, 7.8 us)
Async XLA Ops:
  0.6 5.7 %copy-start.1 = (bf16[2,12,12,1536]{3,0,2,1:T(2,128)(2,1)S(1)}, bf16[2,12,12,1536]{3,0,2,1:T(2,128)(2,1)}, u32[]{:S(2)}) copy-start(bf16[2,12,12,1536]{3,0,2,1:T(2,128)(2,1)} %param.10) | copy-start | bytes 2654212
  0.6 5.4 %copy-start.10 = (s32[2,2]{1,0:T(2,128)S(1)}, s32[2,2]{1,0:T(2,128)}, u32[]{:S(2)}) copy-start(s32[2,2]{1,0:T(2,128)} %param.11) | copy-start | bytes 52
  0.7 4.5 copy-start.3
  36.0 0.6 copy-start.4
  36.0 0.6 copy-start.6
  41.2 189.3 %all-to-all-start = ((bf16[8,36,1536]{2,1,0:T(8,128)(2,1)}), bf16[8,36,1536]{2,1,0:T(8,128)(2,1)}, u32[]{:S(2)}, u32[]{:S(2)}) async-start(bf16[8,36,1536]{2,1,0:T(8,128)(2,1)} %all_to_all.14), calls=%async_computation | async-start | bytes 1966080 | tf_op jit(solution)/shard_map/all_to_all | solution.py:349
  51.3 43.4 %collective-permute-start = (bf16[768,896]{1,0:T(8,128)(2,1)}, bf16[768,896]{1,0:T(8,128)(2,1)}, u32[]{:S(2)}, u32[]{:S(2)}) collective-permute-start(bf16[768,896]{1,0:T(8,128)(2,1)} %constant_dynamic-slice_fusion), channel_id=1, source_target_pairs={{0,4},{2,6},{4,8},{6,10},{8,12},{10,14},{1,5},{3,7},{5,9},{7,11},{... | collective-permute-start | bytes 4128776 | tf_op jit(solution)/shard_map/ppermute | solution.py:317
  55.7 40.5 %collective-permute-start.1 = (bf16[768,896]{1,0:T(8,128)(2,1)}, bf16[768,896]{1,0:T(8,128)(2,1)}, u32[]{:S(2)}, u32[]{:S(2)}) collective-permute-start(bf16[768,896]{1,0:T(8,128)(2,1)} %constant_dynamic-slice_fusion), channel_id=1, source_target_pairs={{4,0},{6,2},{8,4},{10,6},{12,8},{14,10},{5,1},{7,3},{9,5},{11,7},{... | collective-permute-start | bytes 4128776 | tf_op jit(solution)/shard_map/ppermute | solution.py:318
  243.3 1.7 copy-start.11
  244.8 45.6 %collective-permute-start.2 = (bf16[288,3584]{1,0:T(8,128)(2,1)}, bf16[288,3584]{1,0:T(8,128)(2,1)}, u32[]{:S(2)}, u32[]{:S(2)}) collective-permute-start(bf16[288,3584]{1,0:T(8,128)(2,1)} %pad_maximum_fusion), channel_id=1, source_target_pairs={{0,1},{1,0},{2,3},{3,2},{4,5},{5,4},{6,7},{7,6},{8,9},{9,8},{10,11... | collective-permute-start | bytes 6193160 | tf_op jit(solution)/shard_map/ppermute | solution.py:361
  293.7 9.2 %copy-start.8 = (f32[3584]{0:T(1024)S(1)}, f32[3584]{0:T(1024)}, u32[]{:S(2)}) copy-start(f32[3584]{0:T(1024)} %param.18) | copy-start | bytes 43012
  329.1 3.4 copy-start
  329.1 43.4 %collective-permute-start.3 = (bf16[288,3584]{1,0:T(8,128)(2,1)}, bf16[288,3584]{1,0:T(8,128)(2,1)S(1)}, u32[]{:S(2)}, u32[]{:S(2)}) collective-permute-start(bf16[288,3584]{1,0:T(8,128)(2,1)} %gather_fusion), channel_id=1, source_target_pairs={{0,1},{1,0},{2,3},{3,2},{4,5},{5,4},{6,7},{7,6},{8,9},{9,8},{10,11... | collective-permute-start | bytes 6193160 | tf_op jit(solution)/shard_map/ppermute | solution.py:374
  388.3 73.8 %all-to-all-start.1 = ((bf16[8,36,1536]{2,1,0:T(8,128)(2,1)}), bf16[8,36,1536]{2,1,0:T(8,128)(2,1)S(1)}, u32[]{:S(2)}, u32[]{:S(2)}) async-start(bf16[8,36,1536]{2,1,0:T(8,128)(2,1)} %all_to_all.17), calls=%async_computation.1 | async-start | bytes 1966080 | tf_op jit(solution)/shard_map/all_to_all | solution.py:391
  443.4 20.2 %copy-start.5 = (f32[2,12,12]{2,1,0:T(8,128)S(1)}, f32[2,12,12]{2,1,0:T(8,128)}, u32[]{:S(2)}) copy-start(f32[2,12,12]{2,1,0:T(8,128)} %copy-done.4) | copy-start | bytes 3460
  443.4 20.2 %copy-start.7 = (f32[2,12,12]{2,1,0:T(8,128)S(1)}, f32[2,12,12]{2,1,0:T(8,128)}, u32[]{:S(2)}) copy-start(f32[2,12,12]{2,1,0:T(8,128)} %copy-done.6) | copy-start | bytes 3460
  443.4 20.2 %copy-start.9 = (f32[1536]{0:T(1024)S(1)}, f32[1536]{0:T(1024)}, u32[]{:S(2)}) copy-start(f32[1536]{0:T(1024)} %param.13) | copy-start | bytes 18436
  473.3 9.6 %copy-start.2 = (bf16[2,12,12,1536]{3,0,2,1:T(2,128)(2,1)S(1)}, bf16[2,12,12,1536]{3,0,2,1:T(2,128)(2,1)}, u32[]{:S(2)}) copy-start(bf16[2,12,12,1536]{3,0,2,1:T(2,128)(2,1)} %param.10) | copy-start | bytes 2654212

commit v3 on v0

v3 whole, which is shorter than its diff:
```python
import jax
import jax.numpy as jnp
from jax import lax
from jax.experimental import pallas as pl
from jax.experimental.pallas import tpu as pltpu
from jax.sharding import PartitionSpec as P
import functools

MESH = pl.DeviceIdType.MESH


def clip_kernel(
    n_sec, n_tp, entries, delta_ref, out_ref,
    parts, norm_own, norms, scaled, far, part_send, part_recv,
    norm_send, norm_recv, far_sem, all_send, all_recv,
):
    pod = lax.axis_index("outer")
    sec = lax.axis_index("sec")
    tp = lax.axis_index("tp")
    barrier = pltpu.get_barrier_semaphore()
    peers = n_sec * n_tp
    me = tp * n_sec + sec

    def peer(j):
        other = lax.rem(me + j, peers)
        return (pod, other % n_sec, other // n_sec)

    for j in range(1, peers):
        pl.semaphore_signal(barrier, inc=1, device_id=peer(j), device_id_type=MESH)
    pl.semaphore_signal(barrier, inc=1, device_id=(1 - pod, sec, tp), device_id_type=MESH)
    pl.semaphore_wait(barrier, peers)

    def part_copy(j):
        to = lax.rem(sec + j, n_sec)
        return pltpu.make_async_remote_copy(
            src_ref=delta_ref.at[to], dst_ref=parts.at[j - 1],
            send_sem=part_send.at[j - 1], recv_sem=part_recv.at[j - 1],
            device_id=(pod, to, tp), device_id_type=MESH,
        )

    def norm_copy(j):
        return pltpu.make_async_remote_copy(
            src_ref=norm_own, dst_ref=norms.at[j - 1],
            send_sem=norm_send.at[j - 1], recv_sem=norm_recv.at[j - 1],
            device_id=peer(j), device_id_type=MESH,
        )

    def all_copy(j):
        to = lax.rem(sec + j, n_sec)
        return pltpu.make_async_remote_copy(
            src_ref=out_ref.at[sec], dst_ref=out_ref.at[sec],
            send_sem=all_send.at[j - 1], recv_sem=all_recv.at[j - 1],
            device_id=(pod, to, tp), device_id_type=MESH,
        )

    for j in range(1, n_sec):
        part_copy(j).start()
    total = delta_ref[sec]
    for j in range(1, n_sec):
        part_copy(j).wait_recv()
        total = total + parts[j - 1]
    norm_own[...] = jnp.broadcast_to(jnp.sum(total * total, keepdims=True), norm_own.shape)
    for j in range(1, peers):
        norm_copy(j).start()
    square = norm_own[...]
    for j in range(1, peers):
        norm_copy(j).wait_recv()
        square = square + norms[j - 1]
    factor = jnp.minimum(1.0, 1.0 / jnp.sqrt(square / entries + 1e-06))
    scaled[...] = total * factor[0:1, 0:1]
    across = pltpu.make_async_remote_copy(
        src_ref=scaled, dst_ref=far, send_sem=far_sem.at[0], recv_sem=far_sem.at[1],
        device_id=(1 - pod, sec, tp), device_id_type=MESH,
    )
    across.start()
    across.wait()
    out_ref[sec] = (scaled[...] + far[...]) * 0.5
    for j in range(1, n_sec):
        all_copy(j).start()
    for j in range(1, n_sec):
        all_copy(j).wait()
        part_copy(j).wait_send()
    for j in range(1, peers):
        norm_copy(j).wait_send()


def clipped_mean(local_delta):
    n_sec = lax.axis_size("sec")
    n_tp = lax.axis_size("tp")
    rows, width = local_delta.shape
    share = -(-rows // n_sec)
    stacked = jnp.pad(local_delta, ((0, share * n_sec - rows), (0, 0)))
    stacked = stacked.reshape(n_sec, share, width)
    shard = (share, width)
    dma = pltpu.SemaphoreType.DMA
    average = pl.pallas_call(
        functools.partial(clip_kernel, n_sec, n_tp, rows * width * n_tp),
        out_shape=jax.ShapeDtypeStruct(stacked.shape, jnp.float32),
        in_specs=[pl.BlockSpec(memory_space=pltpu.VMEM)],
        out_specs=pl.BlockSpec(memory_space=pltpu.VMEM),
        scratch_shapes=[
            pltpu.VMEM((n_sec - 1,) + shard, jnp.float32),
            pltpu.VMEM((8, 128), jnp.float32),
            pltpu.VMEM((n_sec * n_tp - 1, 8, 128), jnp.float32),
            pltpu.VMEM(shard, jnp.float32),
            pltpu.VMEM(shard, jnp.float32),
            dma((n_sec - 1,)),
            dma((n_sec - 1,)),
            dma((n_sec * n_tp - 1,)),
            dma((n_sec * n_tp - 1,)),
            dma((2,)),
            dma((n_sec - 1,)),
            dma((n_sec - 1,)),
        ],
        compiler_params=pltpu.CompilerParams(
            collective_id=1, has_side_effects=True, vmem_limit_bytes=24 * 1024 * 1024
        ),
    )(stacked)
    return average.reshape(n_sec * share, width)[:rows]


def shape_mask(tile_shape, grid):
    places = lax.broadcasted_iota(jnp.int32, (1, grid), 1)
    rows_ok = places < tile_shape[:, 0:1]
    cols_ok = places < tile_shape[:, 1:2]
    return (rows_ok[:, :, None] & cols_ok[:, None, :]).astype(jnp.float32)


def on_device(
    tile_maps,
    tile_shape,
    conv_kernel,
    norm_gain,
    norm_bias,
    projector,
    text_rows,
    row_order,
    seq_gain,
    cotangent,
):
    grid = tile_maps.shape[1]
    half_ch = tile_maps.shape[3]
    channels = half_ch * lax.axis_size("tp")
    rows_dev = tile_maps.shape[0] * grid * grid
    width = text_rows.shape[1] * lax.axis_size("tp")
    positions = row_order[0, :rows_dev]
    cut = (projector.shape[1] // 2 + 127) // 128 * 128
    near_cols = lax.all_gather(projector[:, :cut], "sec", axis=0, tiled=False)
    rest_cols = lax.all_gather(projector[:, cut:], "sec", axis=0, tiled=False)
    validity = shape_mask(tile_shape, grid)[..., None]
    masked = tile_maps.astype(jnp.float32) * validity
    padded = jnp.pad(masked, ((0, 0), (3, 3), (3, 3), (0, 0)))
    conv_out = jnp.zeros(masked.shape, jnp.float32)
    for row_off in range(7):
        for col_off in range(7):
            conv_out = (
                conv_out
                + padded[:, row_off : row_off + grid, col_off : col_off + grid, :]
                * conv_kernel[row_off, col_off]
            )
    text_wide = text_rows.astype(jnp.float32)
    total_one, total_two, text_square = lax.psum(
        (
            jnp.sum(conv_out, axis=-1),
            jnp.sum(conv_out * conv_out, axis=-1),
            jnp.sum(text_wide * text_wide, axis=-1),
        ),
        "tp",
    )
    center = (total_one / channels)[..., None]
    inverse = lax.rsqrt((total_two / channels)[..., None] - center * center + 1e-06)
    normal = (conv_out - center) * inverse
    features = (
        (validity * (normal * norm_gain + norm_bias))
        .astype(jnp.bfloat16)
        .reshape(rows_dev, half_ch)
    )
    tp_size = lax.axis_size("tp")
    half_width = text_rows.shape[1]
    mine = lax.axis_index("tp")
    swap = [(i, (i + 1) % tp_size) for i in range(tp_size)]
    per_half = near_cols.shape[0] // tp_size

    def halves(weight):
        own = lax.dynamic_slice_in_dim(weight, mine * per_half, per_half, axis=0)
        far = lax.dynamic_slice_in_dim(weight, (1 - mine) * per_half, per_half, axis=0)
        return own, far

    own_near, far_near = halves(near_cols)
    own_rest, far_rest = halves(rest_cols)
    routed = lax.all_to_all(features, "sec", split_axis=0, concat_axis=0, tiled=True)

    def project(rows, weight):
        return [
            jnp.dot(rows, weight[block], preferred_element_type=jnp.float32)
            for block in range(per_half)
        ]

    def summed(own, far):
        sent = jnp.concatenate(
            [part.astype(jnp.bfloat16) for part in project(routed, far)], axis=1
        )
        other = lax.ppermute(sent, "tp", swap)
        step = own.shape[2]
        return [
            (part + other[:, k * step : (k + 1) * step].astype(jnp.float32)).astype(jnp.bfloat16)
            for k, part in enumerate(project(routed, own))
        ]

    near_parts = summed(own_near, far_near)
    rest_parts = summed(own_rest, far_rest)
    arrived = jnp.concatenate(
        [part for pair in zip(near_parts, rest_parts) for part in pair], axis=1
    )
    placed_cotangent = lax.optimization_barrier(cotangent[positions])
    wide = arrived.astype(jnp.float32)
    upstream = placed_cotangent.astype(jnp.float32) * seq_gain
    square_sum, along = lax.psum(
        (jnp.sum(wide * wide, axis=-1), jnp.sum(upstream * wide, axis=-1)), "tp"
    )
    inv_rms = lax.rsqrt(square_sum / width + 1e-05)
    inv_col = inv_rms[:, None]
    picked = (
        inv_col * upstream - wide * (inv_col * inv_col * inv_col) * along[:, None] / width
    ).astype(jnp.bfloat16)
    merged = text_rows.at[positions].set(arrived)
    inv_all = lax.rsqrt(text_square / width + 1e-05).at[positions].set(inv_rms)
    normed = (merged.astype(jnp.float32) * inv_all[:, None] * seq_gain).astype(jnp.bfloat16)
    middle = per_half // 2 * projector.shape[1]
    far_first = lax.ppermute(picked[:, :middle], "tp", swap)
    far_second = lax.ppermute(picked[:, middle:], "tp", swap)

    def project_back(rows, near, rest, first):
        block_width = projector.shape[1]
        total = jnp.zeros((rows.shape[0], half_ch), jnp.float32)
        for k in range(rows.shape[1] // block_width):
            start = k * block_width
            for weight, low, high in (
                (near, start, start + cut),
                (rest, start + cut, start + block_width),
            ):
                total = total + lax.dot_general(
                    rows[:, low:high],
                    weight[first + k],
                    (((1,), (1,)), ((), ())),
                    preferred_element_type=jnp.float32,
                )
        return total

    back = (
        project_back(picked, own_near, own_rest, 0)
        + project_back(far_first, far_near, far_rest, 0)
        + project_back(far_second, far_near, far_rest, per_half // 2)
    ).astype(jnp.bfloat16)
    grad_rows = lax.all_to_all(back, "sec", split_axis=0, concat_axis=0, tiled=True).astype(
        jnp.float32
    )
    masked_grad = grad_rows.reshape(masked.shape) * validity
    scaled = masked_grad * norm_gain
    first_sum, second_sum = lax.psum(
        (jnp.sum(scaled, axis=-1), jnp.sum(scaled * normal, axis=-1)), "tp"
    )
    grad_conv = inverse * (
        scaled - (first_sum / channels)[..., None] - normal * (second_sum / channels)[..., None]
    )
    kernel_rows = []
    for row_off in range(7):
        for col_off in range(7):
            window = padded[:, row_off : row_off + grid, col_off : col_off + grid, :]
            kernel_rows.append(jnp.sum(window * grad_conv, axis=(0, 1, 2)))
    gain_grad = jnp.sum(masked_grad * normal, axis=(0, 1, 2))
    bias_grad = jnp.sum(masked_grad, axis=(0, 1, 2))
    local_delta = jnp.stack(kernel_rows + [gain_grad, bias_grad], axis=0)
    average = clipped_mean(local_delta)
    return (normed, average[:49].reshape(7, 7, half_ch), average[49], average[50])


def solution(mesh):
    in_specs = (
        P(("outer", "sec"), None, None, "tp"),
        P(("outer", "sec"), None),
        P(None, None, "tp"),
        P("tp"),
        P("tp"),
        P("tp", "sec"),
        P(("outer", "sec"), "tp"),
        P(("outer", "sec"), None),
        P("tp"),
        P(("outer", "sec"), "tp"),
    )
    out_specs = (P(("outer", "sec"), "tp"), P(None, None, "tp"), P("tp"), P("tp"))
    return jax.shard_map(
        on_device, mesh=mesh, in_specs=in_specs, out_specs=out_specs, check_vma=False
    )
```

time: 698 us -> 503 us (0.72)
  waiting for transfers between devices: 438 us -> 253 us
  blocking collectives: 80.6 us -> 18.6 us
  Pallas kernels: 0 us -> 31.1 us
  matrix products: 26.4 us -> 48.8 us
  starting transfers between devices: 5.57 us -> 17.2 us
  local copies, waits for them, and re-layouts: 53.2 us -> 43.9 us
  other arithmetic: 78.1 us -> 68.8 us
    reduce_scatter x1 -> x0, waiting for transfers between devices: 95.7 us -> none  [on_device(): lax.psum_scatter(partial_value, 'tp', scatter_dimension=1, tiled=True)]
    all_gather x2, waiting for transfers between devices: 211 us -> 125 us  [the longest x1 111 us: on_device(): near_cols = lax.all_gather(projector[:, :cut], 'sec', axis=0, tiled=False)]
    psum x2 -> x0, waiting for transfers between devices: 78 us -> none  [the longest x1 56.8 us: on_device(): pod_sum = lax.psum(local_delta, 'sec')]
    ppermute x0 -> x4, waiting for transfers between devices: none -> 65.5 us  [the longest x1 40 us: on_device(): far_second = lax.ppermute(picked[:, middle:], 'tp', swap)]
    all_to_all x1 -> x0, blocking collectives: 58.7 us -> none  [on_device(): lax.all_to_all(picked, 'sec', split_axis=0, concat_axis=0, tiled=True)]
    pallas_call x0 -> x1, Pallas kernels: none -> 31.1 us  [clipped_mean(): pl.pallas_call(functools.partial(clip_kernel, n_sec, n_tp, rows * width *...]
    dot_general x2 -> x32, matrix products: 26.4 us -> 48.8 us  [the longest x16 33.9 us: project(): jnp.dot(rows, weight[block], preferred_element_type=jnp.float32)]
    all_to_all x1 -> x2, waiting for transfers between devices: 52.5 us -> 62.9 us  [the longest x1 51 us: on_device(): lax.all_to_all(features, 'sec', split_axis=0, concat_axis=0, tiled=True)]
  transfers between devices with their start and end apart: 6 -> 8, of which waited for: 6 -> 7; matrix products, arithmetic and copies ran while one was open for 5% -> 15% of each run, Pallas kernels for 0% -> 0%
where the time goes in v3:
time: 503 us; the launch traced here: 497 us
  waiting for transfers between devices  253 us (50%)
  other arithmetic  68.8 us (14%)
  matrix products  48.8 us (10%)
  local copies, waits for them, and re-layouts  43.9 us (9%)
  Pallas kernels  31.1 us (6%)
  blocking collectives  18.6 us (4%)
  starting transfers between devices  17.2 us (3%)
  between operations  15.3 us (3%)
    all_gather x1, waiting for transfers between devices, on_device(): near_cols = lax.all_gather(projector[:, :cut], 'sec', axis=0, tiled=False)  111 us
    all_to_all x1, waiting for transfers between devices, on_device(): lax.all_to_all(features, 'sec', split_axis=0, concat_axis=0, tiled=True)  51 us
    ppermute x1, waiting for transfers between devices, on_device(): far_second = lax.ppermute(picked[:, middle:], 'tp', swap)  40 us
    dot_general x16, matrix products, project(): jnp.dot(rows, weight[block], preferred_element_type=jnp.float32)  33.9 us
    pallas_call x1, Pallas kernels, clipped_mean(): pl.pallas_call(functools.partial(clip_kernel, n_sec, n_tp, rows * width *...  31.1 us
    ppermute x2, waiting for transfers between devices, summed(): other = lax.ppermute(sent, 'tp', swap)  25.5 us
    reduce_sum x1, other arithmetic, on_device(): jnp.sum(conv_out, axis=-1)  23.6 us
    reduce_sum x3, other arithmetic, on_device(): kernel_rows.append(jnp.sum(window * grad_conv, axis=(0, 1, 2)))  21.4 us
  transfers between devices with their start and end apart: 8, of which 7 were waited for; matrix products, arithmetic and copies ran while one was open for 15% of the time, Pallas kernels for 0%

profile of v3, /device:TPU:1, one launch (start us, length us, event | category | flops | bytes accessed | tf_op | source)
XLA Modules:
  0.0 496.8 jit_solution(13853092662920129729)
XLA Ops:
  7.2 4.4 copy.28
  11.6 2.4 slice.622
  14.1 2.8 slice.615
  19.0 23.6 %fusion.99 = (f32[2,12,12]{2,1,0:T(8,128)S(1)}, f32[2,12,12]{2,1,0:T(8,128)S(1)}, f32[2,12,12,1536]{3,2,1,0:T(8,128)}) fusion(f32[1536]{0:T(1024)S(1)} %get-tuple-element.110, f32[1536]{0:T(1024)S(1)} %get-tuple-element.111, f32[1536]{0:T(1024)S(1)} %get-tuple-element.64, f32[1536]{0:T(1024)S(1)} %get-tuple-element.65, f32[1536]{0:T(1024)S(1)} %get-tuple-element.66, ...), kind=kLoop, calls=%fused_computation.316 | loop fusion | flops 44236224 | bytes 3842304 | tf_op jit(solution)/shard_map/reduce_sum | solution.py:164
  42.7 8.0 %all-reduce.4 = (f32[2,12,12]{2,1,0:T(8,128)S(1)}, f32[2,12,12]{2,1,0:T(8,128)S(1)}) all-reduce(f32[2,12,12]{2,1,0:T(8,128)S(1)} %get-tuple-element.56, f32[2,12,12]{2,1,0:T(8,128)S(1)} %get-tuple-element.55), channel_id=1, replica_groups=mesh['outer'=2,'sec'=8,'tp'=2] {'tp'}, use_global_device_ids=true, to_apply=%region_3.4 | all-reduce | flops 576 | bytes 4608 | tf_op jit(solution)/shard_map/psum | solution.py:162
  51.3 3.5 multiply_convert_fusion.1
  55.8 7.0 %all-to-all-start = ((bf16[8,36,1536]{2,1,0:T(8,128)(2,1)}), bf16[8,36,1536]{2,1,0:T(8,128)(2,1)S(1)}, u32[]{:S(2)}, u32[]{:S(2)}) async-start(bf16[8,36,1536]{2,1,0:T(8,128)(2,1)} %all_to_all.14), calls=%async_computation | async-start | bytes 1966080 | tf_op jit(solution)/shard_map/all_to_all | solution.py:191
  62.8 51.0 %all-to-all-done = bf16[8,36,1536]{2,1,0:T(8,128)(2,1)S(1)} async-done(((bf16[8,36,1536]{2,1,0:T(8,128)(2,1)}), bf16[8,36,1536]{2,1,0:T(8,128)(2,1)S(1)}, u32[]{:S(2)}, u32[]{:S(2)}) %all-to-all-start) | async-done | bytes 884768 | tf_op jit(solution)/shard_map/all_to_all | solution.py:191
  114.9 13.4 %all-gather.7.cloned.1.call-done = bf16[12288,384]{1,0:T(8,128)(2,1)} async-done(((bf16[1536,384]{1,0:T(8,128)(2,1)}), bf16[12288,384]{1,0:T(8,128)(2,1)}) %all-gather.7.cloned.1.call-update) | async-done | bytes 9437200 | tf_op jit(solution)/shard_map/all_gather | solution.py:149
  128.3 2.8 convolution_convert_fusion
  131.1 2.6 convolution_convert_fusion.1
  133.7 111.3 %all-gather.5.cloned.1.call-done = bf16[12288,512]{1,0:T(8,128)(2,1)} async-done(((bf16[1536,512]{1,0:T(8,128)(2,1)}), bf16[12288,512]{1,0:T(8,128)(2,1)}) %all-gather.5.cloned.1.call-update) | async-done | bytes 12582928 | tf_op jit(solution)/shard_map/all_gather | solution.py:148
  245.0 2.0 fusion.26
  247.1 2.0 fusion.27
  249.1 2.0 fusion.29
  251.2 2.1 fusion.28
  254.7 1.9 convolution_convert_fusion.2
  256.6 1.9 convolution_convert_fusion.3
  261.8 10.2 %gather_fusion = bf16[288,3584]{1,0:T(8,128)(2,1)} fusion(bf16[576,3584]{1,0:T(8,128)(2,1)} %param.19, s32[1024]{0:T(1024)} %pad_clamp_fusion), kind=kCustom, calls=%fused_computation | custom fusion | bytes 4129920 | tf_op jit(solution)/shard_map/gather | solution.py:215
  272.0 8.9 %collective-permute-done = bf16[288,2048]{1,0:T(8,128)(2,1)} collective-permute-done((bf16[288,2048]{1,0:T(8,128)(2,1)S(1)}, bf16[288,2048]{1,0:T(8,128)(2,1)}, u32[]{:S(2)}, u32[]{:S(2)}) %collective-permute-start) | collective-permute-done | bytes 1179680 | tf_op jit(solution)/shard_map/ppermute | solution.py:203
  280.9 2.3 fusion.42
  283.2 16.6 %collective-permute-done.1 = bf16[288,1536]{1,0:T(8,128)(2,1)} collective-permute-done((bf16[288,1536]{1,0:T(8,128)(2,1)}, bf16[288,1536]{1,0:T(8,128)(2,1)}, u32[]{:S(2)}, u32[]{:S(2)}) %collective-permute-start.1) | collective-permute-done | bytes 884768 | tf_op jit(solution)/shard_map/ppermute | solution.py:203
  299.9 1.9 fusion.54
  301.8 2.1 fusion.43
  303.9 2.0 fusion.55
  305.8 2.1 fusion.44
  307.9 2.0 fusion.56
  309.9 2.1 fusion.45
  312.0 2.1 fusion.57
  316.5 4.0 all-reduce.3
  320.5 3.9 fusion.4
  324.4 2.1 fusion.40
  326.5 1.9 fusion.36
  328.4 2.1 fusion.30
  335.9 40.0 %collective-permute-done.3 = bf16[288,1792]{1,0:T(8,128)(2,1)S(1)} collective-permute-done((bf16[288,1792]{1,0:T(8,128)(2,1)S(1)}, bf16[288,1792]{1,0:T(8,128)(2,1)S(1)}, u32[]{:S(2)}, u32[]{:S(2)}) %collective-permute-start.3) | collective-permute-done | bytes 1032224 | tf_op jit(solution)/shard_map/ppermute | solution.py:231
  382.6 7.0 %all-to-all-start.1 = ((bf16[8,36,1536]{2,1,0:T(8,128)(2,1)}), bf16[8,36,1536]{2,1,0:T(8,128)(2,1)S(1)}, u32[]{:S(2)}, u32[]{:S(2)}) async-start(bf16[8,36,1536]{2,1,0:T(8,128)(2,1)} %all_to_all.17), calls=%async_computation.1 | async-start | bytes 1966080 | tf_op jit(solution)/shard_map/all_to_all | solution.py:255
  389.7 3.1 multiply_reduce_fusion
  392.8 9.2 %scatter_fusion = bf16[576,3584]{1,0:T(8,128)(2,1)} fusion(bf16[576,3584]{1,0:T(8,128)(2,1)} %copy.28, s32[288]{0:T(512)S(1)} %copy-done.17, bf16[288,3584]{1,0:T(8,128)(2,1)} %copy-done), kind=kCustom, calls=%fused_computation.1 | custom fusion | bytes 6194304 | tf_op jit(solution)/shard_map/scatter | solution.py:226
  402.0 11.9 %all-to-all-done.1 = bf16[8,36,1536]{2,1,0:T(8,128)(2,1)S(1)} async-done(((bf16[8,36,1536]{2,1,0:T(8,128)(2,1)}), bf16[8,36,1536]{2,1,0:T(8,128)(2,1)S(1)}, u32[]{:S(2)}, u32[]{:S(2)}) %all-to-all-start.1) | async-done | bytes 884768 | tf_op jit(solution)/shard_map/all_to_all | solution.py:255
  414.5 1.5 reshape.175
  416.0 3.4 multiply_reduce_fusion.1
  419.4 6.6 %all-reduce.2 = (f32[576]{0:T(1024)S(1)}, f32[2,12,12]{2,1,0:T(8,128)S(1)}, f32[2,12,12]{2,1,0:T(8,128)S(1)}) all-reduce(f32[576]{0:T(1024)S(1)} %multiply_reduce_fusion, f32[2,12,12]{2,1,0:T(8,128)S(1)} %get-tuple-element.5, f32[2,12,12]{2,1,0:T(8,128)S(1)} %reduce_sum.530), channel_id=1, replica_groups=mesh['outer'=2,'sec'=8,'tp'=2] {'tp'}, use_global_device_ids=true, to_apply=%region_6.7 | all-reduce | flops 1152 | bytes 9216 | tf_op jit(solution)/shard_map/psum | solution.py:162
  426.0 9.6 %multiply_reduce_fusion.2 = (f32[1536]{0:T(1024)S(1)}, f32[1536]{0:T(1024)S(1)}, f32[1536]{0:T(1024)S(1)}, f32[1536]{0:T(1024)S(1)}, f32[1536]{0:T(1024)S(1)}, /...) fusion(f32[2,12,12,1536]{3,2,1,0:T(8,128)S(1)} %convert_multipl, ...), kind=kLoop, calls=%fused_computation.80 | loop fusion | flops 19436544 | bytes 7200384 | tf_op jit(solution)/shard_map/reduce_sum | solution.py:270
  435.6 5.4 %multiply_reduce_fusion.39 = (f32[1536]{0:T(1024)S(1)}, f32[1536]{0:T(1024)S(1)}, f32[1536]{0:T(1024)S(1)}, f32[1536]{0:T(1024)S(1)}, f32[1536]{0:T(1024)S(1)}, ...) fusion(f32[2,12,12,1536]{3,2,1,0:T(8,128)S(1)} %get-tuple-eleme, ...), kind=kLoop, calls=%fused_computation.117 | loop fusion | flops 12366336 | bytes 4504704 | tf_op jit(solution)/shard_map/reduce_sum | solution.py:270
  441.1 6.3 %multiply_reduce_fusion.20 = (f32[1536]{0:T(1024)S(1)}, f32[1536]{0:T(1024)S(1)}, f32[1536]{0:T(1024)S(1)}, f32[1536]{0:T(1024)S(1)}, f32[1536]{0:T(1024)S(1)}, ...) fusion(f32[2,12,12,1536]{3,2,1,0:T(8,128)S(1)} %get-tuple-eleme, ...), kind=kLoop, calls=%fused_computation.98 | loop fusion | flops 15897600 | bytes 3649536 | tf_op jit(solution)/shard_map/reduce_sum | solution.py:270
  448.8 31.1 %shard_map.129 = f32[8,7,1536]{2,1,0:T(8,128)S(1)} custom-call(f32[8,7,1536]{2,1,0:T(8,128)S(1)} %reshape.173.delta_ref), custom_call_target="tpu_custom_call" | custom-call | tf_op jit(solution)/shard_map/pallas_call | solution.py:96
  480.7 2.9 scatter_fusion.1
  484.2 5.5 %multiply_convert_fusion = bf16[576,3584]{1,0:T(8,128)(2,1)} fusion(bf16[576,3584]{1,0:T(8,128)(2,1)} %scatter_fusion, f32[3584]{0:T(1024)S(1)} %copy-done.14, f32[576]{0:T(1024)S(1)} %scatter_fusion.1), kind=kLoop, calls=%fused_computation.51 | loop fusion | flops 8257536 | bytes 8274176 | tf_op jit(solution)/shard_map/convert_element_type | solution.py:228
  (155 shorter events, 26.9 us)
Async XLA Ops:
  7.2 121.1 %all-gather.7.cloned.1.call-start = ((), (), s32[]{:S(2)}) async-start(), calls=%async_computation.3 | async-start | bytes 10616832 | tf_op jit(solution)/shard_map/all_gather | solution.py:149
  14.1 3.0 copy-start.18
  14.1 3.1 copy-start.7
  14.1 4.7 copy-start.2
  14.1 231.0 %all-gather.5.cloned.1.call-start = ((), (), s32[]{:S(2)}) async-start(), calls=%async_computation.2 | async-start | bytes 14155776 | tf_op jit(solution)/shard_map/all_gather | solution.py:148
  50.7 0.6 copy-start.8
  50.7 0.6 copy-start.10
  55.8 58.0 %all-to-all-start = ((bf16[8,36,1536]{2,1,0:T(8,128)(2,1)}), bf16[8,36,1536]{2,1,0:T(8,128)(2,1)S(1)}, u32[]{:S(2)}, u32[]{:S(2)}) async-start(bf16[8,36,1536]{2,1,0:T(8,128)(2,1)} %all_to_all.14), calls=%async_computation | async-start | bytes 1966080 | tf_op jit(solution)/shard_map/all_to_all | solution.py:191
  114.9 16.3 %copy-start.4 = (bf16[288,1536]{1,0:T(8,128)(2,1)S(1)}, bf16[288,1536]{1,0:T(8,128)(2,1)}, u32[]{:S(2)}) copy-start(bf16[288,1536]{1,0:T(8,128)(2,1)} %all_to_all.16) | copy-start | bytes 2654212
  251.1 3.5 copy-start.5
  253.4 27.5 %collective-permute-start = (bf16[288,2048]{1,0:T(8,128)(2,1)S(1)}, bf16[288,2048]{1,0:T(8,128)(2,1)}, u32[]{:S(2)}, u32[]{:S(2)}) collective-permute-start(bf16[288,2048]{1,0:T(8,128)(2,1)S(1)} %pad_maximum_fusion), channel_id=1, source_target_pairs={{0,1},{1,0},{2,3},{3,2},{4,5},{5,4},{6,7},{7,6},{8,9},{9,8},{10,11... | collective-permute-start | bytes 3538952 | tf_op jit(solution)/shard_map/ppermute | solution.py:203
  256.6 2.0 copy-start.12
  256.6 2.0 copy-start.13
  259.6 40.2 %collective-permute-start.1 = (bf16[288,1536]{1,0:T(8,128)(2,1)}, bf16[288,1536]{1,0:T(8,128)(2,1)}, u32[]{:S(2)}, u32[]{:S(2)}) collective-permute-start(bf16[288,1536]{1,0:T(8,128)(2,1)} %pad_maximum_fusion.1), channel_id=1, source_target_pairs={{0,1},{1,0},{2,3},{3,2},{4,5},{5,4},{6,7},{7,6},{8,9},{9,8},{10,11... | collective-permute-start | bytes 2654216 | tf_op jit(solution)/shard_map/ppermute | solution.py:203
  260.6 0.6 copy-start.16
  272.0 27.9 %copy-start.6 = (bf16[288,1536]{1,0:T(8,128)(2,1)S(1)}, bf16[288,1536]{1,0:T(8,128)(2,1)}, u32[]{:S(2)}) copy-start(bf16[288,1536]{1,0:T(8,128)(2,1)} %all_to_all.16) | copy-start | bytes 2654212
  311.9 3.4 copy-start.1
  311.9 3.4 copy-start.14
  314.1 1.3 copy-start
  320.5 10.2 %slice-start = ((s8[12582912]{0:T(1024)(128)(4,1)}), s8[4194304]{0:T(1024)(128)(4,1)S(1)}, s32[]{:S(2)}) async-start(s8[12582912]{0:T(1024)(128)(4,1)} %bitcast.118), calls=%async_computation.4 | async-start | bytes 8388608
  324.4 6.3 %slice-start.1 = ((s8[12582912]{0:T(1024)(128)(4,1)}), s8[4194304]{0:T(1024)(128)(4,1)S(1)}, s32[]{:S(2)}) async-start(s8[12582912]{0:T(1024)(128)(4,1)} %bitcast.118), calls=%async_computation.5 | async-start | bytes 8388608
  328.4 2.5 slice-start.2
  328.4 5.4 %slice-start.3 = ((s8[9437184]{0:T(1024)(128)(4,1)}), s8[4194304]{0:T(1024)(128)(4,1)S(1)}, s32[]{:S(2)}) async-start(s8[9437184]{0:T(1024)(128)(4,1)} %bitcast.139), calls=%async_computation.7 | async-start | bytes 8388608
  330.5 3.3 slice-start.4
  330.9 2.9 slice-start.5
  331.6 46.3 %collective-permute-start.2 = (bf16[288,1792]{1,0:T(8,128)(2,1)S(1)}, bf16[288,1792]{1,0:T(8,128)(2,1)S(1)}, u32[]{:S(2)}, u32[]{:S(2)}) collective-permute-start(bf16[288,1792]{1,0:T(8,128)(2,1)S(1)} %get-tuple-element.123), channel_id=1, source_target_pairs={{0,1},{1,0},{2,3},{3,2},{4,5},{5,4},{6,7},{7,6},{8,9},{9,8},{10,11... | collective-permute-start | bytes 3096584 | tf_op jit(solution)/shard_map/ppermute | solution.py:230
  332.9 43.0 %collective-permute-start.3 = (bf16[288,1792]{1,0:T(8,128)(2,1)S(1)}, bf16[288,1792]{1,0:T(8,128)(2,1)S(1)}, u32[]{:S(2)}, u32[]{:S(2)}) collective-permute-start(bf16[288,1792]{1,0:T(8,128)(2,1)S(1)} %get-tuple-element.124), channel_id=1, source_target_pairs={{0,1},{1,0},{2,3},{3,2},{4,5},{5,4},{6,7},{7,6},{8,9},{9,8},{10,11... | collective-permute-start | bytes 3096584 | tf_op jit(solution)/shard_map/ppermute | solution.py:231
  382.6 31.3 %all-to-all-start.1 = ((bf16[8,36,1536]{2,1,0:T(8,128)(2,1)}), bf16[8,36,1536]{2,1,0:T(8,128)(2,1)S(1)}, u32[]{:S(2)}, u32[]{:S(2)}) async-start(bf16[8,36,1536]{2,1,0:T(8,128)(2,1)} %all_to_all.17), calls=%async_computation.1 | async-start | bytes 1966080 | tf_op jit(solution)/shard_map/all_to_all | solution.py:255
  389.6 3.1 copy-start.17
  392.8 21.2 %copy-start.15 = (f32[1536]{0:T(1024)S(1)}, f32[1536]{0:T(1024)}, u32[]{:S(2)}) copy-start(f32[1536]{0:T(1024)} %param.13) | copy-start | bytes 18436
  402.0 14.0 %copy-start.9 = (f32[2,12,12]{2,1,0:T(8,128)S(1)}, f32[2,12,12]{2,1,0:T(8,128)}, u32[]{:S(2)}) copy-start(f32[2,12,12]{2,1,0:T(8,128)} %copy-done.8) | copy-start | bytes 3460
  402.0 14.0 %copy-start.11 = (f32[2,12,12]{2,1,0:T(8,128)S(1)}, f32[2,12,12]{2,1,0:T(8,128)}, u32[]{:S(2)}) copy-start(f32[2,12,12]{2,1,0:T(8,128)} %copy-done.10) | copy-start | bytes 3460
  426.0 9.6 %copy-start.3 = (bf16[2,12,12,1536]{3,0,2,1:T(2,128)(2,1)S(1)}, bf16[2,12,12,1536]{3,0,2,1:T(2,128)(2,1)}, u32[]{:S(2)}) copy-start(bf16[2,12,12,1536]{3,0,2,1:T(2,128)(2,1)} %param.10) | copy-start | bytes 2654212
Sparse Core Ops, SparseCore 0:
  14.2 114.0 all-gather.6
  129.9 115.0 all-gather.4

commit v4 on v3

--- a/solution.py
+++ b/solution.py
@@ -144,7 +144,7 @@
     rows_dev = tile_maps.shape[0] * grid * grid
     width = text_rows.shape[1] * lax.axis_size("tp")
     positions = row_order[0, :rows_dev]
-    cut = (projector.shape[1] // 2 + 127) // 128 * 128
+    cut = max(128, projector.shape[1] * 2 // 7 // 128 * 128)
     near_cols = lax.all_gather(projector[:, :cut], "sec", axis=0, tiled=False)
     rest_cols = lax.all_gather(projector[:, cut:], "sec", axis=0, tiled=False)
     validity = shape_mask(tile_shape, grid)[..., None]
@@ -178,6 +178,7 @@
     tp_size = lax.axis_size("tp")
     half_width = text_rows.shape[1]
     mine = lax.axis_index("tp")
+    features, text_square = lax.optimization_barrier((features, text_square))
     swap = [(i, (i + 1) % tp_size) for i in range(tp_size)]
     per_half = near_cols.shape[0] // tp_size
 
@@ -186,7 +187,6 @@
         far = lax.dynamic_slice_in_dim(weight, (1 - mine) * per_half, per_half, axis=0)
         return own, far
 
-    own_near, far_near = halves(near_cols)
     own_rest, far_rest = halves(rest_cols)
     routed = lax.all_to_all(features, "sec", split_axis=0, concat_axis=0, tiled=True)
 
@@ -196,7 +196,7 @@
             for block in range(per_half)
         ]
 
-    def summed(own, far):
+    def summed(routed, own, far):
         sent = jnp.concatenate(
             [part.astype(jnp.bfloat16) for part in project(routed, far)], axis=1
         )
@@ -207,8 +207,12 @@
             for k, part in enumerate(project(routed, own))
         ]
 
-    near_parts = summed(own_near, far_near)
-    rest_parts = summed(own_rest, far_rest)
+    rest_parts = summed(routed, own_rest, far_rest)
+    rest_parts, routed_later, near_cols = lax.optimization_barrier(
+        (rest_parts, routed, near_cols)
+    )
+    own_near, far_near = halves(near_cols)
+    near_parts = summed(routed_later, own_near, far_near)
     arrived = jnp.concatenate(
         [part for pair in zip(near_parts, rest_parts) for part in pair], axis=1
     )

time: 503 us -> 452 us (0.90)
  waiting for transfers between devices: 253 us -> 200 us
    all_gather x1, waiting for transfers between devices: 111 us -> 6.42 us  [on_device(): near_cols = lax.all_gather(projector[:, :cut], 'sec', axis=0, tiled=False)]
    all_gather x1, waiting for transfers between devices: 13.4 us -> 62.1 us  [on_device(): rest_cols = lax.all_gather(projector[:, cut:], 'sec', axis=0, tiled=False)]
    ppermute x1, waiting for transfers between devices: 40 us -> 17.8 us  [on_device(): far_second = lax.ppermute(picked[:, middle:], 'tp', swap)]
    ppermute x1, waiting for transfers between devices: 0.01 us -> 19.9 us  [on_device(): far_first = lax.ppermute(picked[:, :middle], 'tp', swap)]
    ppermute x2, waiting for transfers between devices: 25.5 us -> 36.1 us  [summed(): other = lax.ppermute(sent, 'tp', swap)]
    psum x0 -> x1, blocking collectives: none -> 6.53 us  [on_device(): lax.psum((jnp.sum(scaled, axis=-1), jnp.sum(scaled * normal, axis=-1)), '...]
    psum x2 -> x1, blocking collectives: 14.6 us -> 8.67 us  [on_device(): lax.psum((jnp.sum(conv_out, axis=-1), jnp.sum(conv_out * conv_out, axis=-...]
    all_to_all x1, waiting for transfers between devices: 11.9 us -> 6.52 us  [on_device(): lax.all_to_all(back, 'sec', split_axis=0, concat_axis=0, tiled=True)]
  transfers between devices with their start and end apart: 8 -> 8, of which waited for: 7 -> 8; matrix products, arithmetic and copies ran while one was open for 15% -> 20% of each run, Pallas kernels for 0% -> 0%
where the time goes in v4:
time: 452 us; the launch traced here: 445 us
  waiting for transfers between devices  200 us (44%)
  other arithmetic  67.1 us (15%)
  matrix products  51.3 us (11%)
  local copies, waits for them, and re-layouts  43.6 us (10%)
  Pallas kernels  31.1 us (7%)
  blocking collectives  19 us (4%)
  starting transfers between devices  17.6 us (4%)
  between operations  15.4 us (3%)
    all_gather x1, waiting for transfers between devices, on_device(): rest_cols = lax.all_gather(projector[:, cut:], 'sec', axis=0, tiled=False)  62.1 us
    all_to_all x1, waiting for transfers between devices, on_device(): lax.all_to_all(features, 'sec', split_axis=0, concat_axis=0, tiled=True)  51 us
    ppermute x2, waiting for transfers between devices, summed(): other = lax.ppermute(sent, 'tp', swap)  36.1 us
    dot_general x16, matrix products, project(): jnp.dot(rows, weight[block], preferred_element_type=jnp.float32)  35.5 us
    pallas_call x1, Pallas kernels, clipped_mean(): pl.pallas_call(functools.partial(clip_kernel, n_sec, n_tp, rows * width *...  31.1 us
    reduce_sum x1, other arithmetic, on_device(): jnp.sum(conv_out, axis=-1)  22.1 us
    reduce_sum x3, other arithmetic, on_device(): kernel_rows.append(jnp.sum(window * grad_conv, axis=(0, 1, 2)))  21.4 us
    ppermute x1, waiting for transfers between devices, on_device(): far_first = lax.ppermute(picked[:, :middle], 'tp', swap)  19.9 us
  transfers between devices with their start and end apart: 8, of which 8 were waited for; matrix products, arithmetic and copies ran while one was open for 20% of the time, Pallas kernels for 0%

profile of v4, /device:TPU:1, one launch (start us, length us, event | category | flops | bytes accessed | tf_op | source)
XLA Modules:
  0.0 445.0 jit_solution(7425949904455275474)
XLA Ops:
  7.2 4.6 %copy.28 = bf16[576,3584]{1,0:T(8,128)(2,1)} copy(bf16[576,3584]{1,0:T(8,128)(2,1)} %param.16) | data formatting | bytes 8257536
  13.4 2.1 slice.628
  16.7 3.1 multiply_reduce_fusion
  20.0 22.1 %fusion.89 = (f32[2,12,12]{2,1,0:T(8,128)S(1)}, f32[2,12,12]{2,1,0:T(8,128)S(1)}, f32[2,12,12,1536]{3,2,1,0:T(8,128)}) fusion(f32[1536]{0:T(1024)S(1)} %get-tuple-element.126, f32[1536]{0:T(1024)S(1)} %get-tuple-element.127, f32[1536]{0:T(1024)S(1)} %get-tuple-element.80, f32[1536]{0:T(1024)S(1)} %get-tuple-element.81, f32[1536]{0:T(1024)S(1)} %get-tuple-element.82, ...), kind=kLoop, calls=%fused_computation.313 | loop fusion | flops 44236224 | bytes 3842304 | tf_op jit(solution)/shard_map/reduce_sum | solution.py:164
  42.2 8.7 %all-reduce.4 = (f32[2,12,12]{2,1,0:T(8,128)S(1)}, f32[2,12,12]{2,1,0:T(8,128)S(1)}, f32[576]{0:T(1024)}) all-reduce(f32[2,12,12]{2,1,0:T(8,128)S(1)} %get-tuple-element.72, f32[2,12,12]{2,1,0:T(8,128)S(1)} %get-tuple-element.71, f32[576]{0:T(1024)S(1)} %multiply_reduce_fusion), channel_id=1, replica_groups=mesh['outer'=2,'sec'=8,'tp'=2] {'tp'}, use_global_device_ids=true, to_apply=%region_3.4 | all-reduce | flops 1152 | bytes 9216 | tf_op jit(solution)/shard_map/psum | solution.py:162
  51.5 3.5 multiply_convert_fusion.1
  56.1 2.2 all_to_all.14
  58.3 6.9 %all-to-all-start = ((bf16[8,36,1536]{2,1,0:T(8,128)(2,1)}), bf16[8,36,1536]{2,1,0:T(8,128)(2,1)S(1)}, u32[]{:S(2)}, u32[]{:S(2)}) async-start(bf16[8,36,1536]{2,1,0:T(8,128)(2,1)} %all_to_all.14), calls=%async_computation | async-start | bytes 1966080 | tf_op jit(solution)/shard_map/all_to_all | solution.py:191
  65.2 51.0 %all-to-all-done = bf16[8,36,1536]{2,1,0:T(8,128)(2,1)S(1)} async-done(((bf16[8,36,1536]{2,1,0:T(8,128)(2,1)}), bf16[8,36,1536]{2,1,0:T(8,128)(2,1)S(1)}, u32[]{:S(2)}, u32[]{:S(2)}) %all-to-all-start) | async-done | bytes 884768 | tf_op jit(solution)/shard_map/all_to_all | solution.py:191
  117.3 62.1 %all-gather.5.cloned.1.call-done = bf16[12288,640]{1,0:T(8,128)(2,1)} async-done(((bf16[1536,640]{1,0:T(8,128)(2,1)}), bf16[12288,640]{1,0:T(8,128)(2,1)}) %all-gather.5.cloned.1.call-update) | async-done | bytes 15728656 | tf_op jit(solution)/shard_map/all_gather | solution.py:149
  179.5 2.7 fusion.28
  182.1 2.4 fusion.25
  184.6 2.5 fusion.26
  187.1 2.6 fusion.27
  192.0 32.8 %collective-permute-done = bf16[288,2560]{1,0:T(8,128)(2,1)} collective-permute-done((bf16[288,2560]{1,0:T(8,128)(2,1)}, bf16[288,2560]{1,0:T(8,128)(2,1)}, u32[]{:S(2)}, u32[]{:S(2)}) %collective-permute-start) | collective-permute-done | bytes 1474592 | tf_op jit(solution)/shard_map/ppermute | solution.py:203
  224.8 3.2 add_convert_fusion.3
  228.0 3.2 add_convert_fusion
  231.2 3.2 add_convert_fusion.1
  234.4 3.2 add_convert_fusion.2
  237.6 6.4 %all-gather.7.cloned.1.call-done = bf16[12288,256]{1,0:T(8,128)(2,1)} async-done(((bf16[1536,256]{1,0:T(8,128)(2,1)}), bf16[12288,256]{1,0:T(8,128)(2,1)}) %all-gather.7.cloned.1.call-update) | async-done | bytes 6291472 | tf_op jit(solution)/shard_map/all_gather | solution.py:148
  244.0 1.5 convolution_convert_fusion
  245.5 1.5 convolution_convert_fusion.1
  247.1 1.5 convolution_convert_fusion.2
  248.6 1.5 convolution_convert_fusion.3
  252.3 10.5 %gather_fusion = bf16[288,3584]{1,0:T(8,128)(2,1)} fusion(bf16[576,3584]{1,0:T(8,128)(2,1)} %param.19, s32[1024]{0:T(1024)S(1)} %pad_clamp_fusion), kind=kCustom, calls=%fused_computation | custom fusion | bytes 4129920 | tf_op jit(solution)/shard_map/gather | solution.py:219
  262.8 3.3 collective-permute-done.1
  266.0 1.5 fusion.44
  267.7 1.6 fusion.45
  269.4 1.7 fusion.46
  271.1 1.5 fusion.47
  275.1 3.8 all-reduce.3
  278.9 3.9 fusion.4
  282.8 1.7 fusion.29
  284.7 2.6 convolution_add_fusion.8
  287.8 2.6 convolution_add_fusion.6
  294.7 17.8 %collective-permute-done.3 = bf16[288,1792]{1,0:T(8,128)(2,1)S(1)} collective-permute-done((bf16[288,1792]{1,0:T(8,128)(2,1)S(1)}, bf16[288,1792]{1,0:T(8,128)(2,1)S(1)}, u32[]{:S(2)}, u32[]{:S(2)}) %collective-permute-start.3) | collective-permute-done | bytes 1032224 | tf_op jit(solution)/shard_map/ppermute | solution.py:235
  314.8 19.9 %collective-permute-done.2 = bf16[288,1792]{1,0:T(8,128)(2,1)S(1)} collective-permute-done((bf16[288,1792]{1,0:T(8,128)(2,1)S(1)}, bf16[288,1792]{1,0:T(8,128)(2,1)S(1)}, u32[]{:S(2)}, u32[]{:S(2)}) %collective-permute-start.2) | collective-permute-done | bytes 1032224 | tf_op jit(solution)/shard_map/ppermute | solution.py:234
  339.5 6.8 %all-to-all-start.1 = ((bf16[8,36,1536]{2,1,0:T(8,128)(2,1)}), bf16[8,36,1536]{2,1,0:T(8,128)(2,1)S(1)}, u32[]{:S(2)}, u32[]{:S(2)}) async-start(bf16[8,36,1536]{2,1,0:T(8,128)(2,1)} %all_to_all.17), calls=%async_computation.1 | async-start | bytes 1966080 | tf_op jit(solution)/shard_map/all_to_all | solution.py:259
  346.4 9.2 %scatter_fusion = bf16[576,3584]{1,0:T(8,128)(2,1)} fusion(bf16[576,3584]{1,0:T(8,128)(2,1)} %copy.28, s32[288]{0:T(512)S(1)} %fusion.88, bf16[288,3584]{1,0:T(8,128)(2,1)} %copy-done), kind=kCustom, calls=%fused_computation.1 | custom fusion | bytes 6194304 | tf_op jit(solution)/shard_map/scatter | solution.py:230
  355.6 2.9 scatter_fusion.1
  358.5 5.5 %multiply_convert_fusion = bf16[576,3584]{1,0:T(8,128)(2,1)} fusion(bf16[576,3584]{1,0:T(8,128)(2,1)} %scatter_fusion, f32[3584]{0:T(1024)S(1)} %copy-done.15, f32[576]{0:T(1024)S(1)} %scatter_fusion.1), kind=kLoop, calls=%fused_computation.51 | loop fusion | flops 8257536 | bytes 8274176 | tf_op jit(solution)/shard_map/convert_element_type | solution.py:232
  364.1 6.5 %all-to-all-done.1 = bf16[8,36,1536]{2,1,0:T(8,128)(2,1)S(1)} async-done(((bf16[8,36,1536]{2,1,0:T(8,128)(2,1)}), bf16[8,36,1536]{2,1,0:T(8,128)(2,1)S(1)}, u32[]{:S(2)}, u32[]{:S(2)}) %all-to-all-start.1) | async-done | bytes 884768 | tf_op jit(solution)/shard_map/all_to_all | solution.py:259
  372.7 3.4 multiply_reduce_fusion.1
  376.1 6.5 %all-reduce.2 = (f32[2,12,12]{2,1,0:T(8,128)S(1)}, f32[2,12,12]{2,1,0:T(8,128)S(1)}) all-reduce(f32[2,12,12]{2,1,0:T(8,128)S(1)} %get-tuple-element.21, f32[2,12,12]{2,1,0:T(8,128)S(1)} %reduce_sum.530), channel_id=1, replica_groups=mesh['outer'=2,'sec'=8,'tp'=2] {'tp'}, use_global_device_ids=true, to_apply=%region_15.16 | all-reduce | flops 576 | bytes 4608 | tf_op jit(solution)/shard_map/psum | solution.py:264
  382.6 9.6 %multiply_reduce_fusion.2 = (f32[1536]{0:T(1024)S(1)}, f32[1536]{0:T(1024)S(1)}, f32[1536]{0:T(1024)S(1)}, f32[1536]{0:T(1024)S(1)}, f32[1536]{0:T(1024)S(1)}, /...) fusion(f32[2,12,12,1536]{3,2,1,0:T(8,128)S(1)} %convert_multipl, ...), kind=kLoop, calls=%fused_computation.80 | loop fusion | flops 19436544 | bytes 7200384 | tf_op jit(solution)/shard_map/reduce_sum | solution.py:274
  392.3 5.4 %multiply_reduce_fusion.39 = (f32[1536]{0:T(1024)S(1)}, f32[1536]{0:T(1024)S(1)}, f32[1536]{0:T(1024)S(1)}, f32[1536]{0:T(1024)S(1)}, f32[1536]{0:T(1024)S(1)}, ...) fusion(f32[2,12,12,1536]{3,2,1,0:T(8,128)S(1)} %get-tuple-eleme, ...), kind=kLoop, calls=%fused_computation.117 | loop fusion | flops 12366336 | bytes 4504704 | tf_op jit(solution)/shard_map/reduce_sum | solution.py:274
  397.7 6.3 %multiply_reduce_fusion.20 = (f32[1536]{0:T(1024)S(1)}, f32[1536]{0:T(1024)S(1)}, f32[1536]{0:T(1024)S(1)}, f32[1536]{0:T(1024)S(1)}, f32[1536]{0:T(1024)S(1)}, ...) fusion(f32[2,12,12,1536]{3,2,1,0:T(8,128)S(1)} %get-tuple-eleme, ...), kind=kLoop, calls=%fused_computation.98 | loop fusion | flops 15897600 | bytes 3649536 | tf_op jit(solution)/shard_map/reduce_sum | solution.py:274
  405.4 31.1 %shard_map.129 = f32[8,7,1536]{2,1,0:T(8,128)S(1)} custom-call(f32[8,7,1536]{2,1,0:T(8,128)S(1)} %reshape.175.delta_ref), custom_call_target="tpu_custom_call" | custom-call | tf_op jit(solution)/shard_map/pallas_call | solution.py:96
  (162 shorter events, 29.2 us)
Async XLA Ops:
  7.2 172.3 %all-gather.5.cloned.1.call-start = ((), (), s32[]{:S(2)}) async-start(), calls=%async_computation.2 | async-start | bytes 17694720 | tf_op jit(solution)/shard_map/all_gather | solution.py:149
  7.2 4.6 %copy-start.4 = (bf16[1536,896]{1,0:T(8,128)(2,1)S(1)}, bf16[1536,896]{1,0:T(8,128)(2,1)}, u32[]{:S(2)}) copy-start(bf16[1536,896]{1,0:T(8,128)(2,1)} %param.15) | copy-start | bytes 8257540
  13.3 2.2 copy-start.17
  13.3 2.4 copy-start.10
  13.3 230.7 %all-gather.7.cloned.1.call-start = ((), (), s32[]{:S(2)}) async-start(), calls=%async_computation.3 | async-start | bytes 7077888 | tf_op jit(solution)/shard_map/all_gather | solution.py:148
  15.9 3.9 copy-start.2
  50.8 0.6 copy-start.11
  50.9 0.6 copy-start.13
  58.3 57.9 %all-to-all-start = ((bf16[8,36,1536]{2,1,0:T(8,128)(2,1)}), bf16[8,36,1536]{2,1,0:T(8,128)(2,1)S(1)}, u32[]{:S(2)}, u32[]{:S(2)}) async-start(bf16[8,36,1536]{2,1,0:T(8,128)(2,1)} %all_to_all.14), calls=%async_computation | async-start | bytes 1966080 | tf_op jit(solution)/shard_map/all_to_all | solution.py:191
  117.3 64.8 %copy-start.5 = (bf16[288,1536]{1,0:T(8,128)(2,1)S(1)}, bf16[288,1536]{1,0:T(8,128)(2,1)}, u32[]{:S(2)}) copy-start(bf16[288,1536]{1,0:T(8,128)(2,1)} %all_to_all.16) | copy-start | bytes 2654212
  190.9 33.9 %collective-permute-start = (bf16[288,2560]{1,0:T(8,128)(2,1)}, bf16[288,2560]{1,0:T(8,128)(2,1)}, u32[]{:S(2)}, u32[]{:S(2)}) collective-permute-start(bf16[288,2560]{1,0:T(8,128)(2,1)} %pad_maximum_fusion), channel_id=1, source_target_pairs={{0,1},{1,0},{2,3},{3,2},{4,5},{5,4},{6,7},{7,6},{8,9},{9,8},{10,11... | collective-permute-start | bytes 4423688 | tf_op jit(solution)/shard_map/ppermute | solution.py:203
  248.6 3.7 copy-start.19
  251.1 15.0 %collective-permute-start.1 = (bf16[288,1024]{1,0:T(8,128)(2,1)}, bf16[288,1024]{1,0:T(8,128)(2,1)}, u32[]{:S(2)}, u32[]{:S(2)}) collective-permute-start(bf16[288,1024]{1,0:T(8,128)(2,1)} %pad_maximum_fusion.1), channel_id=1, source_target_pairs={{0,1},{1,0},{2,3},{3,2},{4,5},{5,4},{6,7},{7,6},{8,9},{9,8},{10,11... | collective-permute-start | bytes 1769480 | tf_op jit(solution)/shard_map/ppermute | solution.py:203
  262.8 4.8 %copy-start.9 = (bf16[288,640]{1,0:T(8,128)(2,1)S(1)}, bf16[288,640]{1,0:T(8,128)(2,1)}, u32[]{:S(2)}) copy-start(bf16[288,640]{1,0:T(8,128)(2,1)} %add_convert_fusion.3) | copy-start | bytes 1105924
  262.8 6.5 %copy-start.8 = (bf16[288,640]{1,0:T(8,128)(2,1)S(1)}, bf16[288,640]{1,0:T(8,128)(2,1)}, u32[]{:S(2)}) copy-start(bf16[288,640]{1,0:T(8,128)(2,1)} %add_convert_fusion.2) | copy-start | bytes 1105924
  267.7 3.4 copy-start.7
  269.3 3.4 copy-start.6
  269.3 4.7 %copy-start.1 = (bf16[288,3584]{1,0:T(8,128)(2,1)S(1)}, bf16[288,3584]{1,0:T(8,128)(2,1)}, u32[]{:S(2)}) copy-start(bf16[288,3584]{1,0:T(8,128)(2,1)} %gather_fusion) | copy-start | bytes 6193156
  269.4 4.7 %copy-start.15 = (f32[3584]{0:T(1024)S(1)}, f32[3584]{0:T(1024)}, u32[]{:S(2)}) copy-start(f32[3584]{0:T(1024)} %param.18) | copy-start | bytes 43012
  272.7 1.3 copy-start
  278.9 8.4 %slice-start.4 = ((s8[6291456]{0:T(1024)(128)(4,1)}), s8[4194304]{0:T(1024)(128)(4,1)S(1)}, s32[]{:S(2)}) async-start(s8[6291456]{0:T(1024)(128)(4,1)} %bitcast.137), calls=%async_computation.8 | async-start | bytes 8388608
  282.8 9.7 %slice-start = ((s8[15728640]{0:T(1024)(128)(4,1)}), s8[4194304]{0:T(1024)(128)(4,1)S(1)}, s32[]{:S(2)}) async-start(s8[15728640]{0:T(1024)(128)(4,1)} %bitcast.120), calls=%async_computation.4 | async-start | bytes 8388608
  284.6 2.8 slice-start.5
  284.7 7.8 %slice-start.1 = ((s8[15728640]{0:T(1024)(128)(4,1)}), s8[4194304]{0:T(1024)(128)(4,1)S(1)}, s32[]{:S(2)}) async-start(s8[15728640]{0:T(1024)(128)(4,1)} %bitcast.120), calls=%async_computation.5 | async-start | bytes 8388608
  287.3 5.1 %slice-start.2 = ((s8[15728640]{0:T(1024)(128)(4,1)}), s8[4194304]{0:T(1024)(128)(4,1)S(1)}, s32[]{:S(2)}) async-start(s8[15728640]{0:T(1024)(128)(4,1)} %bitcast.120), calls=%async_computation.6 | async-start | bytes 8388608
  287.8 4.7 %slice-start.3 = ((s8[15728640]{0:T(1024)(128)(4,1)}), s8[3145728]{0:T(1024)(128)(4,1)S(1)}, s32[]{:S(2)}) async-start(s8[15728640]{0:T(1024)(128)(4,1)} %bitcast.120), calls=%async_computation.7 | async-start | bytes 6291456
  290.4 22.1 %collective-permute-start.3 = (bf16[288,1792]{1,0:T(8,128)(2,1)S(1)}, bf16[288,1792]{1,0:T(8,128)(2,1)S(1)}, u32[]{:S(2)}, u32[]{:S(2)}) collective-permute-start(bf16[288,1792]{1,0:T(8,128)(2,1)S(1)} %get-tuple-element.140), channel_id=1, source_target_pairs={{0,1},{1,0},{2,3},{3,2},{4,5},{5,4},{6,7},{7,6},{8,9},{9,8},{10,11... | collective-permute-start | bytes 3096584 | tf_op jit(solution)/shard_map/ppermute | solution.py:235
  292.1 42.5 %collective-permute-start.2 = (bf16[288,1792]{1,0:T(8,128)(2,1)S(1)}, bf16[288,1792]{1,0:T(8,128)(2,1)S(1)}, u32[]{:S(2)}, u32[]{:S(2)}) collective-permute-start(bf16[288,1792]{1,0:T(8,128)(2,1)S(1)} %get-tuple-element.139), channel_id=1, source_target_pairs={{0,1},{1,0},{2,3},{3,2},{4,5},{5,4},{6,7},{7,6},{8,9},{9,8},{10,11... | collective-permute-start | bytes 3096584 | tf_op jit(solution)/shard_map/ppermute | solution.py:234
  338.3 8.1 %copy-start.18 = (f32[576]{0:T(1024)S(1)}, f32[576]{0:T(1024)}, u32[]{:S(2)}) copy-start(f32[576]{0:T(1024)} %get-tuple-element.19) | copy-start | bytes 6916
  339.5 31.1 %all-to-all-start.1 = ((bf16[8,36,1536]{2,1,0:T(8,128)(2,1)}), bf16[8,36,1536]{2,1,0:T(8,128)(2,1)S(1)}, u32[]{:S(2)}, u32[]{:S(2)}) async-start(bf16[8,36,1536]{2,1,0:T(8,128)(2,1)} %all_to_all.17), calls=%async_computation.1 | async-start | bytes 1966080 | tf_op jit(solution)/shard_map/all_to_all | solution.py:259
  358.5 12.1 %copy-start.16 = (f32[1536]{0:T(1024)S(1)}, f32[1536]{0:T(1024)}, u32[]{:S(2)}) copy-start(f32[1536]{0:T(1024)} %param.13) | copy-start | bytes 18436
  364.1 8.6 %copy-start.12 = (f32[2,12,12]{2,1,0:T(8,128)S(1)}, f32[2,12,12]{2,1,0:T(8,128)}, u32[]{:S(2)}) copy-start(f32[2,12,12]{2,1,0:T(8,128)} %copy-done.11) | copy-start | bytes 3460
  364.1 8.6 %copy-start.14 = (f32[2,12,12]{2,1,0:T(8,128)S(1)}, f32[2,12,12]{2,1,0:T(8,128)}, u32[]{:S(2)}) copy-start(f32[2,12,12]{2,1,0:T(8,128)} %copy-done.13) | copy-start | bytes 3460
  382.6 9.6 %copy-start.3 = (bf16[2,12,12,1536]{3,0,2,1:T(2,128)(2,1)S(1)}, bf16[2,12,12,1536]{3,0,2,1:T(2,128)(2,1)}, u32[]{:S(2)}) copy-start(bf16[2,12,12,1536]{3,0,2,1:T(2,128)(2,1)} %param.10) | copy-start | bytes 2654212
Sparse Core Ops, SparseCore 0:
  13.5 165.9 all-gather.4
  181.1 62.8 all-gather.6
